TPU v7x, 512 devices: a whole 4x8x8 slice. The times are simulated.
512 devices in a mesh: gx: 8 (over x, core), gy: 8 (over y), gz: 8 (over z).
Axes of the slice: x: 4, y: 8, z: 8, core: 2. Of those that a mesh axis runs over, the one named last changes fastest.
Arguments:
- populations: float32 [19, 32, 128, 1024], P(None, 'gx', 'gy', 'gz'), may hold values from 0.5 to 2
- solid_mask: int32 [32, 128, 1024], P('gx', 'gy', 'gz'), may hold values 0 or 1
- displacement: float32 [3, 524288], P(None, ('gx', 'gy', 'gz')), may hold values from -2 to 2
- stiffness: float32 [524288], P(('gx', 'gy', 'gz')), may hold values from 0.5 to 5
- neighbours: int32 [6, 524288], P(None, ('gx', 'gy', 'gz')), may hold values from 0 to 1023
- owners: int32 [524288, 1], P(('gx', 'gy', 'gz')), may hold values from 0 to 63; in each aligned block of 1024 rows (0 to 1023, 1024 to 2047, ...) at most 32 rows name the same one
- stencil_base: int32 [524288], P(('gx', 'gy', 'gz')), may hold values from 0 to 1660, as said below
- stencil_weights: float32 [12, 524288], P(None, ('gx', 'gy', 'gz')), may hold values from 0.1 to 0.6
Outputs:
- new_populations: float32 [19, 32, 128, 1024], P(None, 'gx', 'gy', 'gz')
- body_force: float32 [3, 32, 128, 1024], P(None, 'gx', 'gy', 'gz')
Inputs may be any that keep to these rules, and one draw needn't show every extreme that they name: `owners`: among the 1024 vertices of one device at most 32 name one brick, a bound that some block reaches. `stencil_base`: each stencil lies wholly inside its owner brick: bx <= 0, by <= 12, bz <= 124.
All inputs are finite; a program needn't handle non-finite values. No bound on the sum of `solid_mask` on one device may be relied on, other than what follows from the above.
Results may differ from a plain program's by a relative error of at most 0.0003.
Values sent between devices are 32-bit elements; how exact they have to be, the bound alone decides.
A program may use at most 64 MiB of HBM per device.

v0:
```python
import math

import jax
import jax.numpy as jnp
import numpy as np
from jax import lax
from jax.sharding import PartitionSpec as P

velocity_x = np.array(
    [0, 1, -1, 0, 0, 0, 0, 1, -1, 1, -1, 1, -1, 1, -1, 0, 0, 0, 0], dtype=np.float32
)
velocity_y = np.array(
    [0, 0, 0, 1, -1, 0, 0, 1, -1, -1, 1, 0, 0, 0, 0, 1, -1, 1, -1], dtype=np.float32
)
velocity_z = np.array(
    [0, 0, 0, 0, 0, 1, -1, 0, 0, 0, 0, 1, -1, -1, 1, 1, -1, -1, 1], dtype=np.float32
)
lattice_weight = np.array([1.0 / 3.0] + [1.0 / 18.0] * 6 + [1.0 / 36.0] * 12, dtype=np.float32)
opposite = np.array([0, 2, 1, 4, 3, 6, 5, 8, 7, 10, 9, 12, 11, 14, 13, 16, 15, 18, 17])
relax_time = 0.8


def extended(cells, sides, width):
    for axis, dim in sides:
        count = lax.axis_size(axis)
        head = lax.slice_in_dim(cells, 0, width, axis=dim)
        tail = lax.slice_in_dim(cells, cells.shape[dim] - width, cells.shape[dim], axis=dim)
        cells = jnp.concatenate(
            [
                lax.ppermute(tail, axis, [(i, (i + 1) % count) for i in range(count)]),
                cells,
                lax.ppermute(head, axis, [((i + 1) % count, i) for i in range(count)]),
            ],
            axis=dim,
        )
    return cells


def collide(shifted, force, solid):
    shape = (19,) + (1,) * (shifted.ndim - 1)
    dir_x = velocity_x.reshape(shape)
    dir_y = velocity_y.reshape(shape)
    dir_z = velocity_z.reshape(shape)
    weight = lattice_weight.reshape(shape)
    density = jnp.sum(shifted, axis=0)
    flow_x = (jnp.sum(dir_x * shifted, axis=0) + 0.5 * force[0]) / density
    flow_y = (jnp.sum(dir_y * shifted, axis=0) + 0.5 * force[1]) / density
    flow_z = (jnp.sum(dir_z * shifted, axis=0) + 0.5 * force[2]) / density
    along = dir_x * flow_x + dir_y * flow_y + dir_z * flow_z
    speed_sq = flow_x * flow_x + flow_y * flow_y + flow_z * flow_z
    equilib = weight * density * (1.0 + 3.0 * along + 4.5 * along * along - 1.5 * speed_sq)
    push = dir_x * force[0] + dir_y * force[1] + dir_z * force[2]
    work = flow_x * force[0] + flow_y * force[1] + flow_z * force[2]
    source = (1.0 - 0.5 / relax_time) * weight * (3.0 * (push - work) + 9.0 * along * push)
    fluid = shifted - (shifted - equilib) / relax_time + source
    return jnp.where(solid[None] == 1, shifted[opposite], fluid)


def axis_table(corner, weights, length):
    offset = jnp.arange(length, dtype=jnp.int32)[:, None] - corner[None, :]
    table = jnp.zeros(offset.shape, jnp.float32)
    for place in range(4):
        table = table + jnp.where(offset == place, weights[place][None, :], 0.0)
    return table


def neighbour_sum(displacement, neighbours):
    count = displacement.shape[1]
    width = math.gcd(count, 512)
    parts = count // width
    vertex_ids = jnp.arange(count, dtype=jnp.int32)[:, None]
    grouped = jnp.transpose(neighbours.reshape(6, parts, width), (1, 0, 2))

    def neighbour_one_block(listed):
        table = jnp.zeros((count, width), jnp.float32)
        for place in range(6):
            table = table + (vertex_ids == listed[place][None, :]).astype(jnp.float32)
        return jnp.dot(
            displacement, table, precision=lax.Precision.HIGHEST, preferred_element_type=jnp.float32
        )

    sums = lax.map(neighbour_one_block, grouped)
    return jnp.transpose(sums, (1, 0, 2)).reshape(3, count)


def owner_ranks(owner, groups):
    count = owner.shape[0]
    brick_ids = jnp.arange(groups, dtype=jnp.int32)
    member = (owner[:, None] == brick_ids[None, :]).astype(jnp.float32)
    tile = math.gcd(count, 128)
    tiles = count // tile
    blocks = member.reshape(tiles, tile, groups)
    inside = jnp.arange(tile, dtype=jnp.int32)
    lower = (inside[:, None] >= inside[None, :]).astype(jnp.float32)
    within = jnp.einsum(
        "ij,bjg->big",
        lower,
        blocks,
        precision=lax.Precision.HIGHEST,
        preferred_element_type=jnp.float32,
    )
    totals = within[:, tile - 1, :]
    across = jnp.arange(tiles, dtype=jnp.int32)
    strict = (across[:, None] > across[None, :]).astype(jnp.float32)
    offsets = jnp.dot(
        strict, totals, precision=lax.Precision.HIGHEST, preferred_element_type=jnp.float32
    )
    running = (within + offsets[:, None, :]).reshape(count, groups)
    return (jnp.sum(running * member, axis=1) - 1.0).astype(jnp.int32)


def place_slots(payload, slot, slots):
    width = math.gcd(slots, 512)
    parts = slots // width
    starts = jnp.arange(parts, dtype=jnp.int32) * width
    columns = jnp.arange(width, dtype=jnp.int32)[None, :]

    def place_one_block(start):
        table = (slot[:, None] == start + columns).astype(jnp.float32)
        return jnp.dot(
            payload, table, precision=lax.Precision.HIGHEST, preferred_element_type=jnp.float32
        )

    placed = lax.map(place_one_block, starts)
    return jnp.transpose(placed, (1, 0, 2)).reshape(payload.shape[0], slots)


def local(
    populations,
    solid_mask,
    displacement,
    stiffness,
    neighbours,
    owners,
    stencil_base,
    stencil_weights,
):
    size_x, size_y, size_z = solid_mask.shape
    count = displacement.shape[1]
    groups = lax.axis_size("gy") * lax.axis_size("gz")
    capacity = 2 * count // groups
    slots = groups * capacity
    vertex_force = stiffness[None, :] * (
        neighbour_sum(displacement, neighbours) - 6.0 * displacement
    )
    owner = owners[:, 0]
    rank_in = owner_ranks(owner, groups)
    slot = owner * capacity + rank_in
    payload = jnp.concatenate(
        [vertex_force, stencil_weights, stencil_base[None, :].astype(jnp.float32)], axis=0
    )
    placed = place_slots(payload, slot, slots)
    send_data = placed[0:15]
    send_base = placed[15:16].astype(jnp.int32)
    got_data, got_base = (
        lax.all_to_all(
            send_data.reshape(15, groups, capacity),
            ("gy", "gz"),
            split_axis=1,
            concat_axis=1,
            tiled=True,
        ),
        lax.all_to_all(
            send_base.reshape(1, groups, capacity),
            ("gy", "gz"),
            split_axis=1,
            concat_axis=1,
            tiled=True,
        ),
    )
    got_data = got_data.reshape(15, slots)
    got_base = got_base.reshape(slots)
    block = math.gcd(slots, 1024)

    def add_block(turn, total):
        start = turn * block
        piece = lax.dynamic_slice_in_dim(got_data, start, block, 1)
        corner = lax.dynamic_slice_in_dim(got_base, start, block, 0)
        table_x = axis_table(corner // (size_y * size_z), piece[3:7], size_x)
        table_y = axis_table(corner // size_z % size_y, piece[7:11], size_y)
        table_z = axis_table(corner % size_z, piece[11:15], size_z)
        left = piece[0:3][:, None, None, :] * table_x[None, :, None, :] * table_y[None, None, :, :]
        left = left.reshape(3 * size_x * size_y, block)
        term = lax.dot_general(
            left,
            table_z,
            (((1,), (1,)), ((), ())),
            precision=lax.Precision.HIGHEST,
            preferred_element_type=jnp.float32,
        )
        return total + term

    total = lax.fori_loop(
        0, slots // block, add_block, jnp.zeros((3 * size_x * size_y, size_z), jnp.float32)
    )
    body_force = total.reshape(3, size_x, size_y, size_z)
    padded = extended(populations, (("gx", 1), ("gy", 2), ("gz", 3)), 1)
    rows = []
    for index in range(19):
        start_x = 1 - int(velocity_x[index])
        start_y = 1 - int(velocity_y[index])
        start_z = 1 - int(velocity_z[index])
        rows.append(
            padded[
                index,
                start_x : start_x + size_x,
                start_y : start_y + size_y,
                start_z : start_z + size_z,
            ]
        )
    shifted = jnp.stack(rows)
    new_populations = collide(shifted, body_force, solid_mask)
    return (new_populations, body_force)


def solution(mesh):
    placed = (
        P(None, "gx", "gy", "gz"),
        P("gx", "gy", "gz"),
        P(None, ("gx", "gy", "gz")),
        P(("gx", "gy", "gz")),
        P(None, ("gx", "gy", "gz")),
        P(("gx", "gy", "gz"), None),
        P(("gx", "gy", "gz")),
        P(None, ("gx", "gy", "gz")),
    )
    return jax.shard_map(
        local,
        mesh=mesh,
        in_specs=placed,
        out_specs=(P(None, "gx", "gy", "gz"), P(None, "gx", "gy", "gz")),
        check_vma=False,
    )
```

profile of v0, /device:TPU:24, one launch (start us, length us, event | category | flops | bytes accessed | tf_op | source)
XLA Modules:
  0.0 111.3 jit_solution(6826323516494897016)
XLA Ops:
  0.6 1.0 fusion.102
  1.7 2.9 %collective-permute-start.1 = (f32[19,1,16,128]{3,2,1,0:T(8,128)S(1)}, f32[19,1,16,128]{3,2,1,0:T(8,128)S(1)}, u32[]{:S(2)}, u32[]{:S(2)}) collective-permute-start(f32[19,1,16,128]{3,2,1,0:T(8,128)S(1)} %get-tuple-element.374), channel_id=1, source_target_pairs={{64,0},{128,64},{192,128},{256,192},{320,256},{384,320},{448,384},... | collective-permute-start | bytes 466952 | tf_op jit(solution)/shard_map/ppermute | solution.py:32
  5.3 0.9 convolution_bitcast_fusion
  6.6 0.8 select_reduce_fusion
  7.5 7.5 %while.41 = (s32[]{:T(128)}, f32[2,3,512]{2,1,0:T(4,128)S(1)}, s32[2,6,512]{2,1,0:T(8,128)}, f32[3,1024]{1,0:T(4,128)S(1)}, s32[]{:T(128)}, /*index=5*/s32[]{:T(128)}, s32[]{}, s32[]{}, s32[]{}, s32[]{}, /*index=10*/s32[]{}) while((s32[]{:T(128)}, f32[2,3,512]{2,1,0:T(4,128)S(1)}, s32[2,6,512]{2,1,0:T(8,128)}, ...), condition=%wide.region_3.4_spmd.clone.clone, body=%wide.region_2.3_spmd.clone.clone.sunk | while | flops 27787272 | bytes 61637 | solution.py:82
  7.5 1.0 constant_dynamic-slice_fusion.9
  8.5 2.8 %fusion.122 = f32[2,3,512]{2,1,0:T(4,128)S(1)} fusion(f32[2,3,512]{2,1,0:T(4,128)S(1)} %get-tuple-element.516, s32[]{:T(128)} %get-tuple-element.515, f32[3,1024]{1,0:T(4,128)S(1)} %get-tuple-element.529, s32[512]{0:T(512)S(1)} %bitcast.180, s32[512]{0:T(512)S(1)} %bitcast.176, s32[512]{0:T(512)S(1)} %bitcast.177, s32[512]{0:T(512)S(1)} %bitcast.178, ...), kind=kOutput, calls=%fused_computation.29.clone.1 | convolution fusion | flops 27787264 | bytes 36868 | tf_op jit(solution)/shard_map/while/body/eval_jaxpr/dot_general | solution.py:78
  11.2 1.0 constant_dynamic-slice_fusion.9
  12.2 2.8 %fusion.122 = f32[2,3,512]{2,1,0:T(4,128)S(1)} fusion(f32[2,3,512]{2,1,0:T(4,128)S(1)} %get-tuple-element.516, s32[]{:T(128)} %get-tuple-element.515, f32[3,1024]{1,0:T(4,128)S(1)} %get-tuple-element.529, s32[512]{0:T(512)S(1)} %bitcast.180, s32[512]{0:T(512)S(1)} %bitcast.176, s32[512]{0:T(512)S(1)} %bitcast.177, s32[512]{0:T(512)S(1)} %bitcast.178, ...), kind=kOutput, calls=%fused_computation.29.clone.1 | convolution fusion | flops 27787264 | bytes 36868 | tf_op jit(solution)/shard_map/while/body/eval_jaxpr/dot_general | solution.py:78
  15.1 8.1 %while.40 = (s32[]{:T(128)}, f32[4,16,512]{2,1,0:T(8,128)S(1)}, s32[1024]{0:T(1024)S(1)}, s32[4]{0:T(128)S(1)}, f32[16,1024]{1,0:T(8,128)S(1)}, /*index=5*/s32[]{:T(128)}) while((s32[]{:T(128)}, f32[4,16,512]{2,1,0:T(8,128)S(1)}, s32[1024]{0:T(1024)S(1)}, s32[4]{0:T(128)S(1)}, f32[16,1024]{1,0:T(8,128)S(1)}, ...), condition=%wide.region_5.6_spmd.clone, body=%wide.region_4.5_spmd.clone.sunk | while | flops 101188096 | bytes 106585 | solution.py:124
  23.9 16.4 %all-to-all-start.1 = ((s32[1,64,32]{2,0,1:T(1,128)}), s32[1,64,32]{2,0,1:T(1,128)S(1)}, u32[]{:S(2)}, u32[]{:S(2)}) async-start(s32[1,64,32]{2,0,1:T(1,128)} %bitcast.13), calls=%async_computation.1 | async-start | bytes 65536 | tf_op jit(solution)/shard_map/all_to_all | solution.py:163
  41.5 0.9 reshape.471
  42.5 7.2 %all-to-all-done.1 = s32[1,64,32]{2,0,1:T(1,128)S(1)} async-done(((s32[1,64,32]{2,0,1:T(1,128)}), s32[1,64,32]{2,0,1:T(1,128)S(1)}, u32[]{:S(2)}, u32[]{:S(2)}) %all-to-all-start.1) | async-done | bytes 8224 | tf_op jit(solution)/shard_map/all_to_all | solution.py:163
  49.6 7.2 %all-to-all-start = ((f32[64,1,480]{2,1,0:T(1,128)}), f32[64,1,480]{2,1,0:T(1,128)S(1)}, u32[]{:S(2)}, u32[]{:S(2)}) async-start(f32[64,1,480]{2,1,0:T(1,128)} %reshape.471), calls=%async_computation | async-start | bytes 262144 | tf_op jit(solution)/shard_map/all_to_all | solution.py:156
  58.3 4.6 %collective-permute-start.2 = (f32[19,6,1,128]{3,2,1,0:T(1,128)S(1)}, f32[19,6,1,128]{3,2,1,0:T(1,128)S(1)}, u32[]{:S(2)}, u32[]{:S(2)}) collective-permute-start(f32[19,6,1,128]{3,2,1,0:T(1,128)S(1)} %get-tuple-element.373), channel_id=1, source_target_pairs={{0,8},{8,16},{16,24},{24,32},{32,40},{40,48},{48,56},{56,0},{1,9},... | collective-permute-start | bytes 175112 | tf_op jit(solution)/shard_map/ppermute | solution.py:30
  62.9 1.9 %collective-permute-start.3 = (f32[19,6,1,128]{3,2,1,0:T(1,128)S(1)}, f32[19,6,1,128]{3,2,1,0:T(1,128)S(1)}, u32[]{:S(2)}, u32[]{:S(2)}) collective-permute-start(f32[19,6,1,128]{3,2,1,0:T(1,128)S(1)} %get-tuple-element.372), channel_id=1, source_target_pairs={{8,0},{16,8},{24,16},{32,24},{40,32},{48,40},{56,48},{0,56},{9,1},... | collective-permute-start | bytes 175112 | tf_op jit(solution)/shard_map/ppermute | solution.py:32
  66.1 4.1 %collective-permute-done.3 = f32[19,6,1,128]{3,2,1,0:T(1,128)S(1)} collective-permute-done((f32[19,6,1,128]{3,2,1,0:T(1,128)S(1)}, f32[19,6,1,128]{3,2,1,0:T(1,128)S(1)}, u32[]{:S(2)}, u32[]{:S(2)}) %collective-permute-start.3) | collective-permute-done | bytes 58400 | tf_op jit(solution)/shard_map/ppermute | solution.py:32
  70.4 1.6 %fusion.100 = (f32[19,6,18,1]{3,2,1,0:T(8,128)S(1)}, f32[19,6,18,1]{3,2,1,0:T(8,128)}) fusion(f32[19,6,18,128]{3,2,1,0:T(8,128)S(1)} %pad_maximum_fusion), kind=kLoop, calls=%fused_computation.186 | loop fusion | bytes 32832 | tf_op jit(solution)/shard_map/slice | solution.py:26
  72.0 2.3 %copy.34 = f32[19,6,18,1]{2,0,3,1:T(8,128)S(1)} copy(f32[19,6,18,1]{3,2,1,0:T(8,128)} %get-tuple-element.371) | data formatting | bytes 16416 | tf_op jit(solution)/shard_map/slice | solution.py:27
  74.3 3.4 %collective-permute-start.4 = (f32[19,6,18,1]{2,0,3,1:T(8,128)S(1)}, f32[19,6,18,1]{2,0,3,1:T(8,128)S(1)}, u32[]{:S(2)}, u32[]{:S(2)}) collective-permute-start(f32[19,6,18,1]{2,0,3,1:T(8,128)S(1)} %copy.34), channel_id=1, source_target_pairs={{0,1},{1,2},{2,3},{3,4},{4,5},{5,6},{6,7},{7,0},{8,9},{9,10},{10,1... | collective-permute-start | bytes 24632 | tf_op jit(solution)/shard_map/ppermute | solution.py:30
  77.6 1.0 copy.36
  78.6 3.8 %collective-permute-start.5 = (f32[19,6,18,1]{2,0,3,1:T(8,128)S(1)}, f32[19,6,18,1]{2,0,3,1:T(8,128)}, u32[]{:S(2)}, u32[]{:S(2)}) collective-permute-start(f32[19,6,18,1]{2,0,3,1:T(8,128)S(1)} %copy.36), channel_id=1, source_target_pairs={{1,0},{2,1},{3,2},{4,3},{5,4},{6,5},{7,6},{0,7},{9,8},{10,9},{11,1... | collective-permute-start | bytes 24632 | tf_op jit(solution)/shard_map/ppermute | solution.py:32
  84.9 2.8 %copy.37 = f32[19,6,18,1]{3,2,1,0:T(8,128)} copy(f32[19,6,18,1]{2,0,3,1:T(8,128)} %collective-permute-done.5) | data formatting | bytes 16416 | tf_op jit(solution)/shard_map/ppermute | solution.py:32
  98.0 1.7 %gather_fusion = f32[19,4,16,128]{3,2,1,0:T(8,128)S(1)} fusion(f32[19,4,16,128]{3,2,1,0:T(8,128)} %get-tuple-element.314, s32[1024]{0:T(1024)S(1)} %pad_clamp_fusion), kind=kCustom, calls=%fused_computation | custom fusion | bytes 1245260 | tf_op jit(solution)/shard_map/gather | solution.py:56
  99.8 0.8 multiply_reduce_fusion.2
  101.1 0.9 reduce.28
  102.7 5.1 %while.42 = (s32[]{:T(128)}, f32[192,128]{1,0:T(8,128)}, f32[15,2048]{1,0:T(8,128)S(1)}, s32[2048]{0:T(1024)S(1)}, s32[]{:T(128)}, /*index=5*/s32[]{:T(128)}, s3...) while((s32[]{:T(128)}, f32[192,128]{1,0:T(8,128)}, ...), condition=%wide.region_7.8_spmd.clone, body=%wide.region_6.7_spmd.clone.sunk | while | flops 304110624 | bytes 2251197 | solution.py:193
  103.2 1.6 %convolution_add_fusion.2 = f32[192,128]{1,0:T(8,128)} fusion(f32[192,1024]{1,0:T(8,128)S(1)} %bitcast.143, f32[1024]{0:T(1024)S(1)} %bitcast.173, f32[1024]{0:T(1024)S(1)} %bitcast.171, f32[1024]{0:T(1024)S(1)} %bitcast.172, f32[1024]{0:T(1024)S(1)} %bitcast.170, s32[1024]{0:T(1024)S(1)} %get-tuple-element.503, f32[192,128]{1,0:T(8,128)} %get-tuple-element.576, ...), kind=kOutput, calls=%fused_computation.42.clone.1 | convolution fusion | flops 303611904 | bytes 1003521 | tf_op jit(solution)/shard_map/while/body/eval_jaxpr/dot_general | solution.py:184
  105.3 2.5 %convolution_add_fusion.2 = f32[192,128]{1,0:T(8,128)} fusion(f32[192,1024]{1,0:T(8,128)S(1)} %bitcast.143, f32[1024]{0:T(1024)S(1)} %bitcast.173, f32[1024]{0:T(1024)S(1)} %bitcast.171, f32[1024]{0:T(1024)S(1)} %bitcast.172, f32[1024]{0:T(1024)S(1)} %bitcast.170, s32[1024]{0:T(1024)S(1)} %get-tuple-element.503, f32[192,128]{1,0:T(8,128)} %get-tuple-element.576, ...), kind=kOutput, calls=%fused_computation.42.clone.1 | convolution fusion | flops 303611904 | bytes 1003521 | tf_op jit(solution)/shard_map/while/body/eval_jaxpr/dot_general | solution.py:184
  107.8 0.8 fusion.103
  108.8 0.9 multiply_bitcast_fusion
  109.8 1.5 %fusion.87 = f32[19,4,16,128]{3,2,1,0:T(8,128)} fusion(f32[19,4,16,128]{3,2,1,0:T(8,128)S(1)} %gather_fusion, f32[19,4,16,128]{3,2,1,0:T(8,128)S(1)} %copy-done.2, f32[4,16,128]{2,1,0:T(8,128)S(1)} %add_bitcast_fusion, f32[4,16,128]{2,1,0:T(8,128)S(1)} %bitcast.148, f32[4,16,128]{2,1,0:T(8,128)S(1)} %bitcast.151, f32[4,16,128]{2,1,0:T(8,128)S(1)} %bitcast.154, ...), kind=kLoop, calls=%fused_computation.111 | loop fusion | flops 4513792 | bytes 2171260 | tf_op jit(solution)/shard_map/jit(_where)/select_n | solution.py:56
  (144 shorter events, 28.7 us)
Async XLA Ops:
  0.6 6.8 %copy-start.17 = (f32[3,1024]{1,0:T(4,128)S(1)}, f32[3,1024]{1,0:T(4,128)}, u32[]{:S(2)}) copy-start(f32[3,1024]{1,0:T(4,128)} %param.23) | copy-start | bytes 36868
  1.7 56.4 %collective-permute-start = (f32[19,1,16,128]{3,2,1,0:T(8,128)S(1)}, f32[19,1,16,128]{3,2,1,0:T(8,128)S(1)}, u32[]{:S(2)}, u32[]{:S(2)}) collective-permute-start(f32[19,1,16,128]{3,2,1,0:T(8,128)S(1)} %get-tuple-element.375), channel_id=1, source_target_pairs={{0,64},{64,128},{128,192},{192,256},{256,320},{320,384},{384,448},... | collective-permute-start | bytes 466952 | tf_op jit(solution)/shard_map/ppermute | solution.py:30
  1.7 56.5 %collective-permute-start.1 = (f32[19,1,16,128]{3,2,1,0:T(8,128)S(1)}, f32[19,1,16,128]{3,2,1,0:T(8,128)S(1)}, u32[]{:S(2)}, u32[]{:S(2)}) collective-permute-start(f32[19,1,16,128]{3,2,1,0:T(8,128)S(1)} %get-tuple-element.374), channel_id=1, source_target_pairs={{64,0},{128,64},{192,128},{256,192},{320,256},{384,320},{448,384},... | collective-permute-start | bytes 466952 | tf_op jit(solution)/shard_map/ppermute | solution.py:32
  7.5 7.5 %copy-start.18 = (s32[1024]{0:T(1024)S(1)}, s32[1024]{0:T(1024)}, u32[]{:S(2)}) copy-start(s32[1024]{0:T(1024)} %param.27) | copy-start | bytes 12292
  7.5 7.5 %copy-start.19 = (f32[1024]{0:T(1024)S(1)}, f32[1024]{0:T(1024)}, u32[]{:S(2)}) copy-start(f32[1024]{0:T(1024)} %param.24) | copy-start | bytes 12292
  7.5 7.5 %copy-start.15 = (f32[12,1024]{1,0:T(8,128)S(1)}, f32[12,1024]{1,0:T(8,128)}, u32[]{:S(2)}) copy-start(f32[12,1024]{1,0:T(8,128)} %param.28) | copy-start | bytes 147460
  15.0 25.3 %copy-start.1 = (f32[19,4,16,128]{3,2,1,0:T(8,128)S(1)}, f32[19,4,16,128]{3,2,1,0:T(8,128)}, u32[]{:S(2)}) copy-start(f32[19,4,16,128]{3,2,1,0:T(8,128)} %param.21) | copy-start | bytes 1867780
  15.0 25.9 %copy-start.16 = (s32[4,16,128]{2,1,0:T(8,128)S(1)}, s32[4,16,128]{2,1,0:T(8,128)}, u32[]{:S(2)}) copy-start(s32[4,16,128]{2,1,0:T(8,128)} %param.22) | copy-start | bytes 98308
  15.0 25.9 %copy-start.26 = (s32[19]{0:T(128)S(1)}, s32[19]{0:T(128)}, u32[]{:S(2)}) copy-start(s32[19]{0:T(128)} %constant.271) | copy-start | bytes 232
  23.9 25.7 %all-to-all-start.1 = ((s32[1,64,32]{2,0,1:T(1,128)}), s32[1,64,32]{2,0,1:T(1,128)S(1)}, u32[]{:S(2)}, u32[]{:S(2)}) async-start(s32[1,64,32]{2,0,1:T(1,128)} %bitcast.13), calls=%async_computation.1 | async-start | bytes 65536 | tf_op jit(solution)/shard_map/all_to_all | solution.py:163
  49.6 51.0 %all-to-all-start = ((f32[64,1,480]{2,1,0:T(1,128)}), f32[64,1,480]{2,1,0:T(1,128)S(1)}, u32[]{:S(2)}, u32[]{:S(2)}) async-start(f32[64,1,480]{2,1,0:T(1,128)} %reshape.471), calls=%async_computation | async-start | bytes 262144 | tf_op jit(solution)/shard_map/all_to_all | solution.py:156
  58.3 7.8 %collective-permute-start.2 = (f32[19,6,1,128]{3,2,1,0:T(1,128)S(1)}, f32[19,6,1,128]{3,2,1,0:T(1,128)S(1)}, u32[]{:S(2)}, u32[]{:S(2)}) collective-permute-start(f32[19,6,1,128]{3,2,1,0:T(1,128)S(1)} %get-tuple-element.373), channel_id=1, source_target_pairs={{0,8},{8,16},{16,24},{24,32},{32,40},{40,48},{48,56},{56,0},{1,9},... | collective-permute-start | bytes 175112 | tf_op jit(solution)/shard_map/ppermute | solution.py:30
  62.9 7.3 %collective-permute-start.3 = (f32[19,6,1,128]{3,2,1,0:T(1,128)S(1)}, f32[19,6,1,128]{3,2,1,0:T(1,128)S(1)}, u32[]{:S(2)}, u32[]{:S(2)}) collective-permute-start(f32[19,6,1,128]{3,2,1,0:T(1,128)S(1)} %get-tuple-element.372), channel_id=1, source_target_pairs={{8,0},{16,8},{24,16},{32,24},{40,32},{48,40},{56,48},{0,56},{9,1},... | collective-permute-start | bytes 175112 | tf_op jit(solution)/shard_map/ppermute | solution.py:32
  74.3 9.5 %collective-permute-start.4 = (f32[19,6,18,1]{2,0,3,1:T(8,128)S(1)}, f32[19,6,18,1]{2,0,3,1:T(8,128)S(1)}, u32[]{:S(2)}, u32[]{:S(2)}) collective-permute-start(f32[19,6,18,1]{2,0,3,1:T(8,128)S(1)} %copy.34), channel_id=1, source_target_pairs={{0,1},{1,2},{2,3},{3,4},{4,5},{5,6},{6,7},{7,0},{8,9},{9,10},{10,1... | collective-permute-start | bytes 24632 | tf_op jit(solution)/shard_map/ppermute | solution.py:30
  78.6 6.3 %collective-permute-start.5 = (f32[19,6,18,1]{2,0,3,1:T(8,128)S(1)}, f32[19,6,18,1]{2,0,3,1:T(8,128)}, u32[]{:S(2)}, u32[]{:S(2)}) collective-permute-start(f32[19,6,18,1]{2,0,3,1:T(8,128)S(1)} %copy.36), channel_id=1, source_target_pairs={{1,0},{2,1},{3,2},{4,3},{5,4},{6,5},{7,6},{0,7},{9,8},{10,9},{11,1... | collective-permute-start | bytes 24632 | tf_op jit(solution)/shard_map/ppermute | solution.py:32
  97.3 2.5 %copy-start.20 = (f32[19]{0:T(128)S(1)}, f32[19]{0:T(128)}, u32[]{:S(2)}) copy-start(f32[19]{0:T(128)} %constant.267) | copy-start | bytes 232
  97.3 2.5 %copy-start.22 = (f32[19]{0:T(128)S(1)}, f32[19]{0:T(128)}, u32[]{:S(2)}) copy-start(f32[19]{0:T(128)} %constant.268) | copy-start | bytes 232
  97.3 2.5 %copy-start.24 = (f32[19]{0:T(128)S(1)}, f32[19]{0:T(128)}, u32[]{:S(2)}) copy-start(f32[19]{0:T(128)} %constant.269) | copy-start | bytes 232
  102.6 6.1 %copy-start.3 = (f32[1,4,16,128]{3,2,1,0:T(8,128)S(1)}, f32[1,4,16,128]{3,2,1,0:T(8,128)}, u32[]{:S(2)}) copy-start(f32[1,4,16,128]{3,2,1,0:T(8,128)} %get-tuple-element.317) | copy-start | bytes 98308
  102.6 6.1 %copy-start.4 = (f32[1,4,16,128]{3,2,1,0:T(8,128)S(1)}, f32[1,4,16,128]{3,2,1,0:T(8,128)}, u32[]{:S(2)}) copy-start(f32[1,4,16,128]{3,2,1,0:T(8,128)} %get-tuple-element.315) | copy-start | bytes 98308
  102.6 6.1 %copy-start.5 = (f32[1,4,16,128]{3,2,1,0:T(8,128)S(1)}, f32[1,4,16,128]{3,2,1,0:T(8,128)}, u32[]{:S(2)}) copy-start(f32[1,4,16,128]{3,2,1,0:T(8,128)} %get-tuple-element.349) | copy-start | bytes 98308
  102.7 6.1 %copy-start.6 = (f32[1,4,16,128]{3,2,1,0:T(8,128)S(1)}, f32[1,4,16,128]{3,2,1,0:T(8,128)}, u32[]{:S(2)}) copy-start(f32[1,4,16,128]{3,2,1,0:T(8,128)} %get-tuple-element.347) | copy-start | bytes 98308
  102.7 6.1 %copy-start.7 = (f32[1,4,16,128]{3,2,1,0:T(8,128)S(1)}, f32[1,4,16,128]{3,2,1,0:T(8,128)}, u32[]{:S(2)}) copy-start(f32[1,4,16,128]{3,2,1,0:T(8,128)} %get-tuple-element.345) | copy-start | bytes 98308
  102.7 6.1 %copy-start.8 = (f32[1,4,16,128]{3,2,1,0:T(8,128)S(1)}, f32[1,4,16,128]{3,2,1,0:T(8,128)}, u32[]{:S(2)}) copy-start(f32[1,4,16,128]{3,2,1,0:T(8,128)} %get-tuple-element.343) | copy-start | bytes 98308
  102.7 6.1 %copy-start.9 = (f32[1,4,16,128]{3,2,1,0:T(8,128)S(1)}, f32[1,4,16,128]{3,2,1,0:T(8,128)}, u32[]{:S(2)}) copy-start(f32[1,4,16,128]{3,2,1,0:T(8,128)} %get-tuple-element.337) | copy-start | bytes 98308
  102.7 6.1 %copy-start.10 = (f32[1,4,16,128]{3,2,1,0:T(8,128)S(1)}, f32[1,4,16,128]{3,2,1,0:T(8,128)}, u32[]{:S(2)}) copy-start(f32[1,4,16,128]{3,2,1,0:T(8,128)} %get-tuple-element.335) | copy-start | bytes 98308
  102.7 6.1 %copy-start.11 = (f32[1,4,16,128]{3,2,1,0:T(8,128)S(1)}, f32[1,4,16,128]{3,2,1,0:T(8,128)}, u32[]{:S(2)}) copy-start(f32[1,4,16,128]{3,2,1,0:T(8,128)} %get-tuple-element.333) | copy-start | bytes 98308
  102.7 6.1 %copy-start.12 = (f32[1,4,16,128]{3,2,1,0:T(8,128)S(1)}, f32[1,4,16,128]{3,2,1,0:T(8,128)}, u32[]{:S(2)}) copy-start(f32[1,4,16,128]{3,2,1,0:T(8,128)} %get-tuple-element.331) | copy-start | bytes 98308
  102.7 6.1 %copy-start.13 = (f32[4,16,128]{2,1,0:T(8,128)S(1)}, f32[4,16,128]{2,1,0:T(8,128)}, u32[]{:S(2)}) copy-start(f32[4,16,128]{2,1,0:T(8,128)} %get-tuple-element.278) | copy-start | bytes 98308
  102.7 6.1 %copy-start.14 = (f32[4,16,128]{2,1,0:T(8,128)S(1)}, f32[4,16,128]{2,1,0:T(8,128)}, u32[]{:S(2)}) copy-start(f32[4,16,128]{2,1,0:T(8,128)} %get-tuple-element.279) | copy-start | bytes 98308
  107.8 1.9 %copy-start.27 = (f32[19]{0:T(128)S(1)}, f32[19]{0:T(128)}, u32[]{:S(2)}) copy-start(f32[19]{0:T(128)} %constant.266) | copy-start | bytes 232
  107.8 1.9 %copy-start.28 = (f32[19]{0:T(128)S(1)}, f32[19]{0:T(128)}, u32[]{:S(2)}) copy-start(f32[19]{0:T(128)} %constant.270) | copy-start | bytes 232
  (5 other events, 8.8 us)
where the time goes:
time: 112 us; the launch traced here: 111 us
  starting transfers between devices  40.4 us (36%)
  local copies, waits for them, and re-layouts  22.3 us (20%)
  other arithmetic  21.8 us (19%)
  matrix products  13.7 us (12%)
  waiting for transfers between devices  11.7 us (10%)
  between operations  1.26 us (1%)
    all_to_all x1, starting transfers between devices, local(): lax.all_to_all(send_base.reshape(1, groups, capacity), ('gy', 'gz'), spli...  16.4 us
    unnamed x18, other arithmetic  11.4 us
    ppermute x3, starting transfers between devices, extended(): lax.ppermute(head, axis, [((i + 1) % count, i) for i in range(count)])  8.71 us
    ppermute x3, starting transfers between devices, extended(): lax.ppermute(tail, axis, [(i, (i + 1) % count) for i in range(count)])  8.02 us
    all_to_all x1, starting transfers between devices, local(): lax.all_to_all(send_data.reshape(15, groups, capacity), ('gy', 'gz'), spl...  7.23 us
    all_to_all x1, waiting for transfers between devices, local(): lax.all_to_all(send_base.reshape(1, groups, capacity), ('gy', 'gz'), spli...  7.16 us
    dot_general x2, matrix products, neighbour_one_block(): jnp.dot(displacement, table, precision=lax.Precision.HIGHEST, preferred_e...  5.52 us
    ppermute x3, waiting for transfers between devices, extended(): lax.ppermute(head, axis, [((i + 1) % count, i) for i in range(count)])  4.5 us
  transfers between devices with their start and end apart: 8, of which 3 were waited for; matrix products, arithmetic and copies ran while one was open for 41% of the time, Pallas kernels for 0%

commit v1 on v0

v1 whole, which is shorter than its diff:
```python
import functools

import jax
import jax.numpy as jnp
import numpy as np
from jax import lax
from jax.experimental import pallas as pl
from jax.experimental.pallas import tpu as pltpu
from jax.sharding import PartitionSpec as P

MESH = pl.DeviceIdType.MESH
F32 = jnp.float32
BF16 = jnp.bfloat16
I32 = jnp.int32

VEL = (
    (0, 0, 0),
    (1, 0, 0), (-1, 0, 0), (0, 1, 0), (0, -1, 0), (0, 0, 1), (0, 0, -1),
    (1, 1, 0), (-1, -1, 0), (1, -1, 0), (-1, 1, 0),
    (1, 0, 1), (-1, 0, -1), (1, 0, -1), (-1, 0, 1),
    (0, 1, 1), (0, -1, -1), (0, 1, -1), (0, -1, 1),
)
SX, SY, SZ = 4, 16, 128
N_GY = N_GZ = 8
GROUP = N_GY * N_GZ
FACE = tuple(
    tuple(tuple(i for i in range(19) if VEL[i][axis] == sign) for sign in (1, -1))
    for axis in range(3)
)
EDGE_XY = (7, 8, 9, 10)
EDGE_XZ = (11, 12, 13, 14)
EDGE_YZ = (15, 16, 17, 18)


def side(sign):
    return 0 if sign > 0 else 1


def face_slot(axis, i):
    s = side(VEL[i][axis])
    return s, FACE[axis][s].index(i)


def bf(x):
    return x.astype(BF16)


def dot_nt(a, b):
    return lax.dot_general(a, b, (((1,), (1,)), ((), ())), preferred_element_type=F32)


def lane_gather(table, index):
    return jnp.take_along_axis(table, index, axis=1, mode="promise_in_bounds")


def pack_faces(pop, hx, hy, hz):
    for s in range(2):
        for k, i in enumerate(FACE[0][s]):
            hx[s, k] = pop[i, 3 if s == 0 else 0]
        row = 15 if s == 0 else 0
        for k, i in enumerate(FACE[1][s]):
            for x in range(SX):
                hy[s, k, x : x + 1, :] = pop[i, x, row : row + 1, :]
        lane = lax.broadcasted_iota(I32, (8, 128), 1)
        edge = 127 if s == 0 else 0
        packed = jnp.zeros((8, 128), F32)
        for k, i in enumerate(FACE[2][s]):
            for x in range(SX):
                for half in range(2):
                    place = 16 * (2 * x + half) + k
                    rolled = pltpu.roll(pop[i, x, 8 * half : 8 * half + 8, :], (place - edge) % 128, 1)
                    packed = jnp.where(lane == place, rolled, packed)
        hz[s] = packed


def pack_vertices(disp, stiff, nbr, owner, base, weights, send, pay):
    lane = lax.broadcasted_iota(I32, (1, 128), 1)
    for v in range(8):
        here = pl.ds(128 * v, 128)
        index = nbr[:, here]
        low, high = index & 127, index >> 7
        for c in range(3):
            total = jnp.zeros((6, 128), F32)
            for k in range(8):
                table = jnp.broadcast_to(disp[c : c + 1, 128 * k : 128 * k + 128], (6, 128))
                total = jnp.where(high == k, lane_gather(table, low), total)
            summed = jnp.sum(total, axis=0, keepdims=True)
            pay[c : c + 1, here] = stiff[:, here] * (summed - 6.0 * disp[c : c + 1, here])
        pay[3:4, here] = base[:, here].astype(F32)
    own = owner[...]
    group_ids = lax.broadcasted_iota(I32, (GROUP, 128), 0)
    member = [jnp.where(own[:, 128 * v : 128 * v + 128] == group_ids, 1.0, 0.0) for v in range(8)]
    before = [jnp.zeros((GROUP, 128), F32)]
    for v in range(7):
        before.append(before[v] + member[v])
    stacked = jnp.concatenate(
        [jnp.concatenate([bf(member[v]), bf(before[v])], axis=1) for v in range(8)], axis=0
    )
    rows = lax.broadcasted_iota(I32, (256, 128), 0)
    cols = lax.broadcasted_iota(I32, (256, 128), 1)
    upto = bf(jnp.where((rows <= cols) | (rows >= 128), 1.0, 0.0))
    running = jnp.dot(stacked, upto, preferred_element_type=F32)
    quad_ids = lax.broadcasted_iota(I32, (GROUP // 4, 128), 0)
    slot_ids = lax.broadcasted_iota(I32, (128, 128), 0)
    lefts, rights = [], []
    for v in range(8):
        rank = jnp.sum(member[v] * running[GROUP * v : GROUP * v + GROUP], axis=0, keepdims=True) - 1.0
        own_v = own[:, 128 * v : 128 * v + 128]
        slot = (own_v & 3) * 32 + rank.astype(I32)
        quad = (own_v >> 2) == quad_ids
        lefts.append(
            jnp.concatenate(
                [
                    bf(jnp.where(quad, lane.astype(F32), 0.0)),
                    bf(jnp.where(quad, float(v + 1), 0.0)),
                ],
                axis=0,
            )
        )
        rights.append(bf(jnp.where(slot == slot_ids, 1.0, 0.0)))
    found = dot_nt(jnp.concatenate(lefts, axis=1), jnp.concatenate(rights, axis=1))
    found = found.astype(I32)
    low, high = found[0:16], found[16:32] - 1
    lows = [low] + [pltpu.roll(low, 32 * j, 1) for j in range(1, 4)]
    highs = [high] + [pltpu.roll(high, 32 * j, 1) for j in range(1, 4)]
    lane_quad = lax.broadcasted_iota(I32, (16, 128), 1) >> 5
    for r in range(4):
        picked = []
        for pl_ in range(4):
            p = 4 * r + pl_
            got = jnp.zeros((16, 128), F32)
            for k in range(8):
                if p < 4:
                    row = pay[p : p + 1, 128 * k : 128 * k + 128]
                else:
                    row = weights[p - 4 : p - 3, 128 * k : 128 * k + 128]
                table = jnp.broadcast_to(row, (16, 128))
                got = jnp.where(highs[pl_] == k, lane_gather(table, lows[pl_]), got)
            picked.append(got)
        for q in range(4):
            mixed = picked[0]
            for pl_ in range(1, 4):
                mixed = jnp.where(lane_quad == (q + pl_) % 4, picked[pl_], mixed)
            if q:
                mixed = pltpu.roll(mixed, 128 - 32 * q, 1)
            send[pl.ds(4 * q + r, 16, stride=16), :] = mixed


def prep_kernel(pop, disp, stiff, nbr, owner, base, weights, send, hx, hy, hz, pay):
    pack_faces(pop, hx, hy, hz)
    pack_vertices(disp, stiff, nbr, owner, base, weights, send, pay)


def halo_messages(hx, hy, hz, got_hx, got_hy, got_hz, got_xy, got_xz, got_yz):
    messages = []
    for s, sign in enumerate((1, -1)):
        messages.append(((sign, 0, 0), hx.at[s], got_hx.at[s]))
        messages.append(((0, sign, 0), hy.at[s], got_hy.at[s]))
        messages.append(((0, 0, sign), hz.at[s], got_hz.at[s]))
    for n, i in enumerate(EDGE_XY):
        s, k = face_slot(1, i)
        messages.append((VEL[i], hy.at[s, k], got_xy.at[n]))
    for n, i in enumerate(EDGE_XZ):
        s, k = face_slot(0, i)
        messages.append((VEL[i], hx.at[s, k], got_xz.at[n]))
    for n, i in enumerate(EDGE_YZ):
        s, k = face_slot(1, i)
        messages.append((VEL[i], hy.at[s, k], got_yz.at[n]))
    return messages


def exchange_kernel(
    send, hx, hy, hz, got, got_hx, got_hy, got_hz, got_xy, got_xz, got_yz,
    send_sem, recv_sem, halo_send, halo_recv, own_sem,
):
    gx, gy, gz = lax.axis_index("gx"), lax.axis_index("gy"), lax.axis_index("gz")
    me = gy * N_GZ + gz

    def device(dx, dy, dz):
        return {
            "gx": lax.rem(gx + dx + 8, 8),
            "gy": lax.rem(gy + dy + N_GY, N_GY),
            "gz": lax.rem(gz + dz + N_GZ, N_GZ),
        }

    messages = halo_messages(hx, hy, hz, got_hx, got_hy, got_hz, got_xy, got_xz, got_yz)
    barrier = pltpu.get_barrier_semaphore()
    outside = [m[0] for m in messages if m[0][0] != 0]
    for step in outside:
        pl.semaphore_signal(barrier, inc=1, device_id=device(*step), device_id_type=MESH)

    def greet(t, carry):
        pl.semaphore_signal(
            barrier, inc=1, device_id=device(0, t // N_GZ, lax.rem(t, N_GZ)), device_id_type=MESH
        )
        return carry

    lax.fori_loop(1, GROUP, greet, 0)
    pl.semaphore_wait(barrier, GROUP - 1 + len(outside))

    own = pltpu.make_async_copy(send.at[me], got.at[me], own_sem)
    own.start()
    halos = []
    for n, (step, src, dst) in enumerate(messages):
        copy = pltpu.make_async_remote_copy(
            src_ref=src, dst_ref=dst, send_sem=halo_send.at[n], recv_sem=halo_recv.at[n],
            device_id=device(*step), device_id_type=MESH,
        )
        copy.start()
        halos.append(copy)

    def vertex_copy(t, outgoing):
        dy, dz = t // N_GZ, lax.rem(t, N_GZ)
        if outgoing:
            there = device(0, dy, dz)
            index, slot = there["gy"] * N_GZ + there["gz"], me
        else:
            there = device(0, N_GY - dy, N_GZ - dz)
            index = slot = there["gy"] * N_GZ + there["gz"]
        return pltpu.make_async_remote_copy(
            src_ref=send.at[index], dst_ref=got.at[slot],
            send_sem=send_sem.at[t], recv_sem=recv_sem.at[t],
            device_id=there, device_id_type=MESH,
        )

    def start(t, carry):
        vertex_copy(t, True).start()
        return carry

    def finish_in(t, carry):
        vertex_copy(t, False).wait_recv()
        return carry

    def finish_out(t, carry):
        vertex_copy(t, True).wait_send()
        return carry

    lax.fori_loop(1, GROUP, start, 0)
    for copy in halos:
        copy.wait()
    own.wait()
    lax.fori_loop(1, GROUP, finish_in, 0)
    lax.fori_loop(1, GROUP, finish_out, 0)


def spread(got, force, quads, left, table):
    lane_quad = lax.broadcasted_iota(I32, (16, 128), 1) >> 5
    for r in range(4):
        skewed = []
        for j in range(4):
            block = got[pl.ds(4 * j + r, 16, stride=16), :]
            skewed.append(pltpu.roll(block, 32 * j, 1) if j else block)
        for pl_ in range(4):
            mixed = skewed[0]
            for j in range(1, 4):
                mixed = jnp.where(lane_quad == (pl_ + j) % 4, skewed[j], mixed)
            if pl_:
                mixed = pltpu.roll(mixed, 128 - 32 * pl_, 1)
            quads[4 * r + pl_] = mixed
    iota_y = lax.broadcasted_iota(I32, (SY, 128), 0).astype(F32)
    iota_z = lax.broadcasted_iota(I32, (SZ, 128), 0).astype(F32)
    for g in range(16):
        here = pl.ds(128 * g, 128)

        def row(p):
            return quads[p, g : g + 1, :]

        corner = row(3).astype(I32)
        corner_y, corner_z = (corner >> 7).astype(F32), (corner & 127).astype(F32)
        off_y = iota_y - corner_y
        off_z = iota_z - corner_z
        table_y = jnp.zeros((SY, 128), F32)
        for j in range(4):
            table_y = jnp.where(off_y == float(j), row(8 + j), table_y)
        high = jnp.zeros((SZ, 128), F32)
        low = jnp.zeros((SZ, 128), F32)
        for k in range(4):
            weight = row(12 + k)
            weight_high = bf(weight).astype(F32)
            hit = off_z == float(k)
            high = jnp.where(hit, weight_high, high)
            low = jnp.where(hit, weight - weight_high, low)
        table[0:SZ, here] = bf(high)
        table[SZ : 2 * SZ, here] = bf(low)
        for c in range(3):
            for x in range(SX):
                value = (row(c) * row(4 + x)) * table_y
                value_high = bf(value)
                place = (c * SX + x) * SY
                left[place : place + SY, here] = value_high
                left[192 + place : 192 + place + SY, here] = bf(value - value_high.astype(F32))
    out = dot_nt(left[...], table[...])
    total = out[0:192, 0:SZ] + (out[192:384, 0:SZ] + out[0:192, SZ : 2 * SZ])
    for c in range(3):
        for x in range(SX):
            place = (c * SX + x) * SY
            force[c, x] = total[place : place + SY]


def moved(pop, halos, i, x, masks):
    hx, hy, hz, exy, exz, eyz = halos
    cx, cy, cz = VEL[i]
    source = x - cx
    inside = 0 <= source < SX
    if inside:
        cells = pop[i, source]
    else:
        cells = hx[face_slot(0, i)]
    if cz:
        cells = pltpu.roll(cells, cz % 128, 1)
        s, k = face_slot(2, i)
        edge = 0 if cz > 0 else 127
        if inside:
            packed = hz[s]
            column = jnp.concatenate(
                [pltpu.roll(packed, (edge - 16 * (2 * source + half) - k) % 128, 1) for half in range(2)],
                axis=0,
            )
        else:
            column = pltpu.roll(exz[EDGE_XZ.index(i)], cz % 128, 1)
        cells = jnp.where(masks["z", cz], column, cells)
    if cy:
        cells = pltpu.roll(cells, cy % 16, 0)
        if inside:
            line = hy[face_slot(1, i)]
            if cz:
                line = pltpu.roll(line, cz % 128, 1)
                beyond = pltpu.roll(eyz[EDGE_YZ.index(i)], cz % 128, 1)
                line = jnp.where(masks["z4", cz], beyond, line)
        else:
            line = exy[EDGE_XY.index(i)]
        line = line[source % SX : source % SX + 1]
        cells = jnp.where(masks["y", cy], jnp.broadcast_to(line, (SY, SZ)), cells)
    return cells


def collide(pop, solid, force, halos, new):
    lane = lax.broadcasted_iota(I32, (SY, SZ), 1)
    line = lax.broadcasted_iota(I32, (SY, SZ), 0)
    lane4 = lax.broadcasted_iota(I32, (SX, SZ), 1)
    masks = {
        ("z", 1): lane == 0, ("z", -1): lane == SZ - 1,
        ("z4", 1): lane4 == 0, ("z4", -1): lane4 == SZ - 1,
        ("y", 1): line == 0, ("y", -1): line == SY - 1,
    }
    for x in range(SX):
        s = [moved(pop, halos, i, x, masks) for i in range(19)]
        density = s[0]
        momentum = [None, None, None]
        for i in range(1, 19, 2):
            density = density + (s[i] + s[i + 1])
            gap = s[i] - s[i + 1]
            for axis in range(3):
                c = VEL[i][axis]
                if c:
                    old = momentum[axis]
                    if old is None:
                        momentum[axis] = gap
                    else:
                        momentum[axis] = old + gap if c > 0 else old - gap
        push = [force[c, x] for c in range(3)]
        inverse = 1.0 / density
        flow = [(momentum[a] + 0.5 * push[a]) * inverse for a in range(3)]
        speed = flow[0] * flow[0] + flow[1] * flow[1] + flow[2] * flow[2]
        work = flow[0] * push[0] + flow[1] * push[1] + flow[2] * push[2]
        wall = solid[x] == 1
        common = density * (1.25 - 1.875 * speed) - 1.125 * work
        square = 5.625 * density
        linear = 3.75 * density
        new[0, x] = jnp.where(wall, s[0], (1.0 / 3.0) * common - 0.25 * s[0])
        for i in range(1, 19, 2):
            weight = 1.0 / 18.0 if i < 7 else 1.0 / 36.0
            a = b = None
            for axis in range(3):
                c = VEL[i][axis]
                if c:
                    if a is None:
                        a, b = flow[axis], push[axis]
                    elif c > 0:
                        a, b = a + flow[axis], b + push[axis]
                    else:
                        a, b = a - flow[axis], b - push[axis]
            even = weight * (common + a * (square * a + 3.375 * b))
            odd = weight * (linear * a + 1.125 * b)
            new[i, x] = jnp.where(wall, s[i + 1], (even + odd) - 0.25 * s[i])
            new[i + 1, x] = jnp.where(wall, s[i], (even - odd) - 0.25 * s[i + 1])


def lattice_kernel(
    pop, solid, got, hx, hy, hz, exy, exz, eyz, new, force, quads, left, table
):
    spread(got, force, quads, left, table)
    collide(pop, solid, force, (hx, hy, hz, exy, exz, eyz), new)


def whole(count):
    return [pl.BlockSpec(memory_space=pltpu.VMEM)] * count


def local(populations, solid_mask, displacement, stiffness, neighbours, owners, stencil_base, stencil_weights):
    def f32(*shape):
        return jax.ShapeDtypeStruct(shape, F32)

    halo_shapes = (f32(2, 5, SY, SZ), f32(2, 5, SX, SZ), f32(2, 8, 128))
    send, hx, hy, hz = pl.pallas_call(
        prep_kernel,
        out_shape=(f32(256, 128),) + halo_shapes,
        in_specs=whole(7),
        out_specs=tuple(whole(4)),
        scratch_shapes=[pltpu.VMEM((4, 1024), F32)],
        name="prepare",
    )(
        populations, displacement, stiffness.reshape(1, 1024), neighbours,
        owners.reshape(1, 1024), stencil_base.reshape(1, 1024), stencil_weights,
    )
    received = pl.pallas_call(
        exchange_kernel,
        out_shape=(f32(GROUP, 4, 128),) + halo_shapes + (f32(4, SX, SZ), f32(4, SY, SZ), f32(4, SX, SZ)),
        in_specs=whole(4),
        out_specs=tuple(whole(7)),
        scratch_shapes=[
            pltpu.SemaphoreType.DMA((GROUP,)),
            pltpu.SemaphoreType.DMA((GROUP,)),
            pltpu.SemaphoreType.DMA((18,)),
            pltpu.SemaphoreType.DMA((18,)),
            pltpu.SemaphoreType.DMA,
        ],
        compiler_params=pltpu.CompilerParams(collective_id=0, has_side_effects=True),
        name="exchange",
    )(send.reshape(GROUP, 4, 128), hx, hy, hz)
    got, halos = received[0], received[1:]
    return tuple(
        pl.pallas_call(
            lattice_kernel,
            out_shape=(f32(19, SX, SY, SZ), f32(3, SX, SY, SZ)),
            in_specs=whole(9),
            out_specs=tuple(whole(2)),
            scratch_shapes=[
                pltpu.VMEM((16, 16, 128), F32),
                pltpu.VMEM((384, 2048), BF16),
                pltpu.VMEM((256, 2048), BF16),
            ],
            compiler_params=pltpu.CompilerParams(vmem_limit_bytes=24 * 1024 * 1024),
            name="lattice",
        )(populations, solid_mask, got.reshape(256, 128), *halos)
    )


def solution(mesh):
    placed = (
        P(None, "gx", "gy", "gz"),
        P("gx", "gy", "gz"),
        P(None, ("gx", "gy", "gz")),
        P(("gx", "gy", "gz")),
        P(None, ("gx", "gy", "gz")),
        P(("gx", "gy", "gz"), None),
        P(("gx", "gy", "gz")),
        P(None, ("gx", "gy", "gz")),
    )
    return jax.shard_map(
        local,
        mesh=mesh,
        in_specs=placed,
        out_specs=(P(None, "gx", "gy", "gz"), P(None, "gx", "gy", "gz")),
        check_vma=False,
    )
```

time: 112 us -> 39.7 us (0.35)
  the two profiles are of different devices: /device:TPU:24 before, /device:TPU:4 now
where the time goes in v1:
time: 39.7 us; the launch traced here: 39.2 us
  Pallas kernels  33.2 us (84%)
  local copies, waits for them, and re-layouts  5.34 us (13%)
  between operations  0.68 us (2%)
    pallas_call x1, Pallas kernels, local(): pl.pallas_call(exchange_kernel, out_shape=(f32(GROUP, 4, 128),) + halo_sh...  27.2 us
    unnamed x18, local copies, waits for them, and re-layouts  5.34 us
    pallas_call x1, Pallas kernels, local(): pl.pallas_call(prep_kernel, out_shape=(f32(256, 128),) + halo_shapes, in_...  3.04 us
    pallas_call x1, Pallas kernels, local(): pl.pallas_call(lattice_kernel, out_shape=(f32(19, SX, SY, SZ), f32(3, SX,...  2.92 us

profile of v1, /device:TPU:4, one launch (start us, length us, event | category | flops | bytes accessed | tf_op | source)
XLA Modules:
  0.0 39.2 jit_solution(1145203904973675909)
XLA Ops:
  0.6 0.0 copy-start
  0.6 3.0 %prepare.1 = (f32[256,128]{1,0:T(8,128)}, f32[2,5,16,128]{3,2,1,0:T(8,128)}, f32[2,5,4,128]{3,2,1,0:T(4,128)}, f32[2,8,128]{2,1,0:T(8,128)}) custom-call(f32[19,4,16,128]{3,2,1,0:T(8,128)} %pop.3, f32[3,1024]{1,0:T(4,128)} %disp.1, f32[1,1024]{1,0:T(1,128)} %bitcast.7, s32[6,1024]{1,0:T(8,128)} %nbr.1, s32[1,1024]{1,0:T(1,128)} %bitcast.8, ...), custom_call_target="tpu_custom_call" | custom-call | tf_op jit(solution)/shard_map/prepare/pallas_call | solution.py:405
  3.7 0.0 copy-start.3
  3.7 27.2 %exchange.1 = (f32[64,4,128]{2,1,0:T(4,128)}, f32[2,5,16,128]{3,2,1,0:T(8,128)}, f32[2,5,4,128]{3,2,1,0:T(4,128)}, f32[2,8,128]{2,1,0:T(8,128)}, f32[4,4,128]{2,...) custom-call(f32[64,4,128]{2,1,0:T(4,128)} %bitcast.6, f32[2,5,16,128]{3,2,1,0:T(8,128)} %get-tuple-element.14.hx, ...), custom_call_target="tpu_custom_call" | custom-call | tf_op jit(solution)/shard_map/exchange/pallas_call | solution.py:416
  30.9 0.0 copy-start.6
  30.9 0.0 copy-done
  30.9 0.0 copy-done.3
  30.9 0.7 %copy-done.6 = f32[2,8,128]{2,1,0:T(8,128)S(1)} copy-done((f32[2,8,128]{2,1,0:T(8,128)S(1)}, f32[2,8,128]{2,1,0:T(8,128)}, u32[]{:S(2)}) %copy-start.6) | copy-done | bytes 8216
  31.6 0.0 copy-start.1
  31.6 0.9 %copy-done.1 = f32[64,4,128]{2,1,0:T(4,128)S(1)} copy-done((f32[64,4,128]{2,1,0:T(4,128)S(1)}, f32[64,4,128]{2,1,0:T(4,128)}, u32[]{:S(2)}) %copy-start.1) | copy-done | bytes 131096
  32.5 0.0 copy-start.2
  32.5 0.9 %copy-done.2 = f32[2,5,16,128]{3,2,1,0:T(8,128)S(1)} copy-done((f32[2,5,16,128]{3,2,1,0:T(8,128)S(1)}, f32[2,5,16,128]{3,2,1,0:T(8,128)}, u32[]{:S(2)}) %copy-start.2) | copy-done | bytes 81944
  33.4 0.0 copy-start.4
  33.4 0.8 %copy-done.4 = f32[4,16,128]{2,1,0:T(8,128)S(1)} copy-done((f32[4,16,128]{2,1,0:T(8,128)S(1)}, f32[4,16,128]{2,1,0:T(8,128)}, u32[]{:S(2)}) %copy-start.4) | copy-done | bytes 32792
  34.2 0.0 copy-start.5
  34.2 0.7 %copy-done.5 = f32[2,5,4,128]{3,2,1,0:T(4,128)S(1)} copy-done((f32[2,5,4,128]{3,2,1,0:T(4,128)S(1)}, f32[2,5,4,128]{3,2,1,0:T(4,128)}, u32[]{:S(2)}) %copy-start.5) | copy-done | bytes 20504
  34.9 0.0 copy-start.7
  34.9 0.7 %copy-done.7 = f32[4,4,128]{2,1,0:T(4,128)S(1)} copy-done((f32[4,4,128]{2,1,0:T(4,128)S(1)}, f32[4,4,128]{2,1,0:T(4,128)}, u32[]{:S(2)}) %copy-start.7) | copy-done | bytes 8216
  35.6 0.0 copy-start.8
  35.6 0.7 %copy-done.8 = f32[4,4,128]{2,1,0:T(4,128)S(1)} copy-done((f32[4,4,128]{2,1,0:T(4,128)S(1)}, f32[4,4,128]{2,1,0:T(4,128)}, u32[]{:S(2)}) %copy-start.8) | copy-done | bytes 8216
  36.3 2.9 %lattice.1 = (f32[19,4,16,128]{3,2,1,0:T(8,128)}, f32[3,4,16,128]{3,2,1,0:T(8,128)}) custom-call(f32[19,4,16,128]{3,2,1,0:T(8,128)S(1)} %copy-done, s32[4,16,128]{2,1,0:T(8,128)S(1)} %copy-done.3, f32[256,128]{1,0:T(8,128)S(1)} %bitcast.5, f32[2,5,16,128]{3,2,1,0:T(8,128)S(1)} %copy-done.2, f32[2,5,4,128]{3,2,1,0:T(4,128)S(1)} %copy-done.5, ...), custom_call_target="tpu_custom_call" | custom-call | tf_op jit(solution)/shard_map/lattice/pallas_call | solution.py:433
Async XLA Ops:
  0.6 30.3 %copy-start = (f32[19,4,16,128]{3,2,1,0:T(8,128)S(1)}, f32[19,4,16,128]{3,2,1,0:T(8,128)}, u32[]{:S(2)}) copy-start(f32[19,4,16,128]{3,2,1,0:T(8,128)} %pop.3) | copy-start | bytes 1867780
  3.7 27.2 %copy-start.3 = (s32[4,16,128]{2,1,0:T(8,128)S(1)}, s32[4,16,128]{2,1,0:T(8,128)}, u32[]{:S(2)}) copy-start(s32[4,16,128]{2,1,0:T(8,128)} %solid.1) | copy-start | bytes 98308
  30.9 0.7 %copy-start.6 = (f32[2,8,128]{2,1,0:T(8,128)S(1)}, f32[2,8,128]{2,1,0:T(8,128)}, u32[]{:S(2)}) copy-start(f32[2,8,128]{2,1,0:T(8,128)} %get-tuple-element.20.hz) | copy-start | bytes 24580
  31.6 0.9 %copy-start.1 = (f32[64,4,128]{2,1,0:T(4,128)S(1)}, f32[64,4,128]{2,1,0:T(4,128)}, u32[]{:S(2)}) copy-start(f32[64,4,128]{2,1,0:T(4,128)} %get-tuple-element.17) | copy-start | bytes 393220
  32.5 0.9 %copy-start.2 = (f32[2,5,16,128]{3,2,1,0:T(8,128)S(1)}, f32[2,5,16,128]{3,2,1,0:T(8,128)}, u32[]{:S(2)}) copy-start(f32[2,5,16,128]{3,2,1,0:T(8,128)} %get-tuple-element.18.hx) | copy-start | bytes 245764
  33.4 0.8 %copy-start.4 = (f32[4,16,128]{2,1,0:T(8,128)S(1)}, f32[4,16,128]{2,1,0:T(8,128)}, u32[]{:S(2)}) copy-start(f32[4,16,128]{2,1,0:T(8,128)} %get-tuple-element.22.exz) | copy-start | bytes 98308
  34.2 0.7 %copy-start.5 = (f32[2,5,4,128]{3,2,1,0:T(4,128)S(1)}, f32[2,5,4,128]{3,2,1,0:T(4,128)}, u32[]{:S(2)}) copy-start(f32[2,5,4,128]{3,2,1,0:T(4,128)} %get-tuple-element.19.hy) | copy-start | bytes 61444
  34.9 0.7 %copy-start.7 = (f32[4,4,128]{2,1,0:T(4,128)S(1)}, f32[4,4,128]{2,1,0:T(4,128)}, u32[]{:S(2)}) copy-start(f32[4,4,128]{2,1,0:T(4,128)} %get-tuple-element.21.exy) | copy-start | bytes 24580
  35.6 0.7 %copy-start.8 = (f32[4,4,128]{2,1,0:T(4,128)S(1)}, f32[4,4,128]{2,1,0:T(4,128)}, u32[]{:S(2)}) copy-start(f32[4,4,128]{2,1,0:T(4,128)} %get-tuple-element.23.eyz) | copy-start | bytes 24580

commit v2 on v1

v2 whole, which is shorter than its diff:
```python
import functools

import jax
import jax.numpy as jnp
import numpy as np
from jax import lax
from jax.experimental import pallas as pl
from jax.experimental.pallas import tpu as pltpu
from jax.sharding import PartitionSpec as P

MESH = pl.DeviceIdType.MESH
F32 = jnp.float32
BF16 = jnp.bfloat16
I32 = jnp.int32

VEL = (
    (0, 0, 0),
    (1, 0, 0), (-1, 0, 0), (0, 1, 0), (0, -1, 0), (0, 0, 1), (0, 0, -1),
    (1, 1, 0), (-1, -1, 0), (1, -1, 0), (-1, 1, 0),
    (1, 0, 1), (-1, 0, -1), (1, 0, -1), (-1, 0, 1),
    (0, 1, 1), (0, -1, -1), (0, 1, -1), (0, -1, 1),
)
SX, SY, SZ = 4, 16, 128
N_GY = N_GZ = 8
GROUP = N_GY * N_GZ
FACE = tuple(
    tuple(tuple(i for i in range(19) if VEL[i][axis] == sign) for sign in (1, -1))
    for axis in range(3)
)
EDGE_XY = (7, 8, 9, 10)
EDGE_XZ = (11, 12, 13, 14)
EDGE_YZ = (15, 16, 17, 18)


def side(sign):
    return 0 if sign > 0 else 1


def face_slot(axis, i):
    s = side(VEL[i][axis])
    return s, FACE[axis][s].index(i)


def bf(x):
    return x.astype(BF16)


def dot_nt(a, b):
    return lax.dot_general(a, b, (((1,), (1,)), ((), ())), preferred_element_type=F32)


def lane_gather(table, index):
    return jnp.take_along_axis(table, index, axis=1, mode="promise_in_bounds")


def pack_faces(pop, hx, hy, hz):
    for s in range(2):
        for k, i in enumerate(FACE[0][s]):
            hx[s, k] = pop[i, 3 if s == 0 else 0]
        row = 15 if s == 0 else 0
        for k, i in enumerate(FACE[1][s]):
            for x in range(SX):
                hy[s, k, x : x + 1, :] = pop[i, x, row : row + 1, :]
        lane = lax.broadcasted_iota(I32, (8, 128), 1)
        edge = 127 if s == 0 else 0
        packed = jnp.zeros((8, 128), F32)
        for k, i in enumerate(FACE[2][s]):
            for x in range(SX):
                for half in range(2):
                    place = 16 * (2 * x + half) + k
                    rolled = pltpu.roll(pop[i, x, 8 * half : 8 * half + 8, :], (place - edge) % 128, 1)
                    packed = jnp.where(lane == place, rolled, packed)
        hz[s] = packed


def pack_vertices(disp, stiff, nbr, owner, base, weights, send, pay):
    lane = lax.broadcasted_iota(I32, (1, 128), 1)
    own = owner[...]
    group_ids = lax.broadcasted_iota(I32, (GROUP, 128), 0)
    member = [jnp.where(own[:, 128 * v : 128 * v + 128] == group_ids, 1.0, 0.0) for v in range(8)]
    before = [jnp.zeros((GROUP, 128), F32)]
    for v in range(7):
        before.append(before[v] + member[v])
    stacked = jnp.concatenate(
        [jnp.concatenate([bf(member[v]), bf(before[v])], axis=1) for v in range(8)], axis=0
    )
    rows = lax.broadcasted_iota(I32, (256, 128), 0)
    cols = lax.broadcasted_iota(I32, (256, 128), 1)
    upto = bf(jnp.where((rows <= cols) | (rows >= 128), 1.0, 0.0))
    running = jnp.dot(stacked, upto, preferred_element_type=F32)
    for v in range(8):
        here = slice(128 * v, 128 * v + 128)
        index = nbr[:, here]
        low, high = index & 127, index >> 7
        for c in range(3):
            total = jnp.zeros((6, 128), F32)
            for k in range(8):
                table = jnp.broadcast_to(disp[c : c + 1, 128 * k : 128 * k + 128], (6, 128))
                total = jnp.where(high == k, lane_gather(table, low), total)
            summed = jnp.sum(total, axis=0, keepdims=True)
            value = stiff[:, here] * (summed - 6.0 * disp[c : c + 1, here])
            pay[c, 0:1, here] = value
            pay[c, 4:5, here] = value
        value = base[:, here].astype(F32)
        pay[3, 0:1, here] = value
        pay[3, 4:5, here] = value
    for l in range(4):
        for i in range(3):
            value = weights[4 * i + l : 4 * i + l + 1, :]
            pay[l, i + 1 : i + 2, :] = value
            pay[l, i + 5 : i + 6, :] = value
    quad_ids = lax.broadcasted_iota(I32, (GROUP // 4, 128), 0)
    slot_ids = lax.broadcasted_iota(I32, (128, 128), 0)
    lefts, rights = [], []
    for v in range(8):
        rank = jnp.sum(member[v] * running[GROUP * v : GROUP * v + GROUP], axis=0, keepdims=True) - 1.0
        own_v = own[:, 128 * v : 128 * v + 128]
        slot = (own_v & 3) * 32 + rank.astype(I32)
        quad = (own_v >> 2) == quad_ids
        lefts.append(
            jnp.concatenate(
                [
                    bf(jnp.where(quad, lane.astype(F32), 0.0)),
                    bf(jnp.where(quad, float(v + 1), 0.0)),
                ],
                axis=0,
            )
        )
        rights.append(bf(jnp.where(slot == slot_ids, 1.0, 0.0)))
    found = dot_nt(jnp.concatenate(lefts, axis=1), jnp.concatenate(rights, axis=1))
    code = (found[0:16] + 128.0 * found[16:32]).astype(I32)
    codes = [code] + [pltpu.roll(code, 32 * j, 1) for j in range(1, 4)]
    lane_quad = lax.broadcasted_iota(I32, (8, 128), 1) >> 5
    for h in range(8):
        picked = []
        for l in range(4):
            pair = jnp.concatenate(
                [jnp.broadcast_to(codes[l][g : g + 1], (4, 128)) for g in (2 * h, 2 * h + 1)], axis=0
            )
            low, high = pair & 127, pair >> 7
            got = jnp.zeros((8, 128), F32)
            for k in range(8):
                got = jnp.where(high == k + 1, lane_gather(pay[l, :, 128 * k : 128 * k + 128], low), got)
            picked.append(got)
        for q in range(4):
            mixed = picked[0]
            for l in range(1, 4):
                mixed = jnp.where(lane_quad == (q + l) % 4, picked[l], mixed)
            if q:
                mixed = pltpu.roll(mixed, 128 - 32 * q, 1)
            send[8 * h + q] = mixed[0:4]
            send[8 * h + 4 + q] = mixed[4:8]


def spread_step(got, sources, quads, left, table):
    lane_quad = lax.broadcasted_iota(I32, (4, 128), 1) >> 5
    iota_y = lax.broadcasted_iota(I32, (SY, 128), 0).astype(F32)
    iota_z = lax.broadcasted_iota(I32, (SZ, 128), 0).astype(F32)
    for n, g in enumerate(sources):
        here = slice(128 * n, 128 * n + 128)
        skewed = [got[4 * g + j] for j in range(4)]
        skewed = [pltpu.roll(skewed[j], 32 * j, 1) if j else skewed[j] for j in range(4)]
        for l in range(4):
            mixed = skewed[0]
            for j in range(1, 4):
                mixed = jnp.where(lane_quad == (l + j) % 4, skewed[j], mixed)
            if l:
                mixed = pltpu.roll(mixed, 128 - 32 * l, 1)
            quads[g, l] = mixed

        def row(p):
            return quads[g, p % 4, p // 4 : p // 4 + 1, :]

        corner = row(3).astype(I32)
        off_y = iota_y - (corner >> 7).astype(F32)
        off_z = iota_z - (corner & 127).astype(F32)
        table_y = jnp.zeros((SY, 128), F32)
        for j in range(4):
            table_y = jnp.where(off_y == float(j), row(8 + j), table_y)
        high = jnp.zeros((SZ, 128), F32)
        low = jnp.zeros((SZ, 128), F32)
        for k in range(4):
            weight = row(12 + k)
            weight_high = bf(weight).astype(F32)
            hit = off_z == float(k)
            high = jnp.where(hit, weight_high, high)
            low = jnp.where(hit, weight - weight_high, low)
        table[0:SZ, here] = bf(high)
        table[SZ : 2 * SZ, here] = bf(low)
        for c in range(3):
            for x in range(SX):
                value = (row(c) * row(4 + x)) * table_y
                value_high = bf(value)
                place = (c * SX + x) * SY
                left[place : place + SY, here] = value_high
                left[192 + place : 192 + place + SY, here] = bf(value - value_high.astype(F32))
    return dot_nt(left[...], table[...])


def moved(pop, halos, i, x, masks):
    hx, hy, hz, exy, exz, eyz = halos
    cx, cy, cz = VEL[i]
    source = x - cx
    inside = 0 <= source < SX
    if inside:
        cells = pop[i, source]
    else:
        cells = hx[face_slot(0, i)]
    if cz:
        cells = pltpu.roll(cells, cz % 128, 1)
        s, k = face_slot(2, i)
        edge = 0 if cz > 0 else 127
        if inside:
            packed = hz[s]
            column = jnp.concatenate(
                [pltpu.roll(packed, (edge - 16 * (2 * source + half) - k) % 128, 1) for half in range(2)],
                axis=0,
            )
        else:
            column = pltpu.roll(exz[EDGE_XZ.index(i)], cz % 128, 1)
        cells = jnp.where(masks["z", cz], column, cells)
    if cy:
        cells = pltpu.roll(cells, cy % 16, 0)
        if inside:
            line = hy[face_slot(1, i)]
            if cz:
                line = pltpu.roll(line, cz % 128, 1)
                beyond = pltpu.roll(eyz[EDGE_YZ.index(i)], cz % 128, 1)
                line = jnp.where(masks["z4", cz], beyond, line)
        else:
            line = exy[EDGE_XY.index(i)]
        line = line[source % SX : source % SX + 1]
        cells = jnp.where(masks["y", cy], jnp.broadcast_to(line, (SY, SZ)), cells)
    return cells


def halo_messages(hx, hy, hz, got_hx, got_hy, got_hz, got_xy, got_xz, got_yz):
    messages = []
    for s, sign in enumerate((1, -1)):
        messages.append(((sign, 0, 0), hx.at[s], got_hx.at[s]))
        messages.append(((0, sign, 0), hy.at[s], got_hy.at[s]))
        messages.append(((0, 0, sign), hz.at[s], got_hz.at[s]))
    for n, i in enumerate(EDGE_XY):
        s, k = face_slot(1, i)
        messages.append((VEL[i], hy.at[s, k], got_xy.at[n]))
    for n, i in enumerate(EDGE_XZ):
        s, k = face_slot(0, i)
        messages.append((VEL[i], hx.at[s, k], got_xz.at[n]))
    for n, i in enumerate(EDGE_YZ):
        s, k = face_slot(1, i)
        messages.append((VEL[i], hy.at[s, k], got_yz.at[n]))
    return messages


def gather_kernel(
    pop_hbm, disp, stiff, nbr, owner, base, weights, shifted, force,
    pop, pay, send, got, hx, hy, hz, got_hx, got_hy, got_hz, got_xy, got_xz, got_yz,
    quads, left, table, total,
    load_sem, send_sem, recv_sem, halo_send, halo_recv, late_sem,
):
    gx, gy, gz = lax.axis_index("gx"), lax.axis_index("gy"), lax.axis_index("gz")
    me = gy * N_GZ + gz
    first = gz < 4

    def place(dx, dy, dz):
        return {
            "gx": lax.rem(gx + dx + 8, 8),
            "gy": lax.rem(gy + dy + N_GY, N_GY),
            "gz": lax.rem(gz + dz + N_GZ, N_GZ),
        }

    def signal(semaphore, device):
        pl.semaphore_signal(semaphore, inc=1, device_id=device, device_id_type=MESH)

    messages = halo_messages(hx, hy, hz, got_hx, got_hy, got_hz, got_xy, got_xz, got_yz)
    barrier = pltpu.get_barrier_semaphore()
    outside = [m[0] for m in messages if m[0][0] != 0]

    @pl.when(first)
    def _():
        for t in range(1, GROUP):
            signal(barrier, place(0, t // N_GZ, t % N_GZ))

    for step in outside:
        signal(barrier, place(*step))
    load = pltpu.make_async_copy(pop_hbm, pop, load_sem)
    load.start()

    pack_vertices(disp, stiff, nbr, owner, base, weights, send, pay)

    @pl.when(first)
    def _():
        pl.semaphore_wait(barrier, 31 + len(outside))

    @pl.when(jnp.logical_not(first))
    def _():
        pl.semaphore_wait(barrier, 32 + len(outside))
        for k in range(8):
            for z in range(4):
                signal(late_sem, {"gx": gx, "gy": lax.rem(gy + k, N_GY), "gz": z})

    def vertex_copy(y, z):
        index = y * N_GZ + z
        return pltpu.make_async_remote_copy(
            src_ref=send.at[index], dst_ref=got.at[me],
            send_sem=send_sem.at[index], recv_sem=recv_sem.at[me],
            device_id={"gx": gx, "gy": y, "gz": z}, device_id_type=MESH,
        )

    def vertex_copies(planes, act):
        for z in planes:
            for k in range(8):
                copy = vertex_copy(lax.rem(gy + k, N_GY), z)
                if k:
                    act(copy)
                else:
                    pl.when(gz != z)(functools.partial(act, copy))

    vertex_copies(range(0, 4), lambda copy: copy.start())
    own = pltpu.make_async_copy(send.at[me], got.at[me], recv_sem.at[me])
    own.start()

    load.wait()
    pack_faces(pop, hx, hy, hz)
    halos = []
    for n, (step, src, dst) in enumerate(messages):
        halos.append(
            pltpu.make_async_remote_copy(
                src_ref=src, dst_ref=dst, send_sem=halo_send.at[n], recv_sem=halo_recv.at[n],
                device_id=place(*step), device_id_type=MESH,
            )
        )

    def start_halos(late):
        for (step, _, _), copy in zip(messages, halos):
            if step[0]:
                if not late:
                    copy.start()
            else:
                near = lax.rem(gz + step[2] + N_GZ, N_GZ) < 4
                pl.when(jnp.logical_not(near) if late else near)(copy.start)

    start_halos(False)

    def arrived(y, z):
        index = y * N_GZ + z
        pltpu.make_async_copy(send.at[index], got.at[index], recv_sem.at[index]).wait()

    order = ((0, 1), (2, 3), (7, 6), (5, 4))

    def step(n, half):
        for y in order[n]:
            for z in range(4 * half, 4 * half + 4):
                arrived(y, z)
        return spread_step(got, [2 * y + half for y in order[n]], quads, left, table)

    total[...] = step(0, 0)
    for n in range(1, 4):
        total[...] += step(n, 0)

    @pl.when(first)
    def _():
        pl.semaphore_wait(late_sem, 32)

    vertex_copies(range(4, 8), lambda copy: copy.start())
    start_halos(True)

    for copy in halos:
        copy.wait_recv()
    lane = lax.broadcasted_iota(I32, (SY, SZ), 1)
    line = lax.broadcasted_iota(I32, (SY, SZ), 0)
    lane4 = lax.broadcasted_iota(I32, (SX, SZ), 1)
    masks = {
        ("z", 1): lane == 0, ("z", -1): lane == SZ - 1,
        ("z4", 1): lane4 == 0, ("z4", -1): lane4 == SZ - 1,
        ("y", 1): line == 0, ("y", -1): line == SY - 1,
    }
    received = (got_hx, got_hy, got_hz, got_xy, got_xz, got_yz)
    for x in range(SX):
        for i in range(19):
            shifted[i, x] = moved(pop, received, i, x, masks)

    for n in range(3):
        total[...] += step(n, 1)
    for copy in halos:
        copy.wait_send()
    vertex_copies(range(8), lambda copy: copy.wait_send())
    last = total[...] + step(3, 1)
    field = last[0:192, 0:SZ] + (last[192:384, 0:SZ] + last[0:192, SZ : 2 * SZ])
    for c in range(3):
        for x in range(SX):
            spot = (c * SX + x) * SY
            force[c, x] = field[spot : spot + SY]


def collide_kernel(shifted, solid, body, new, force):
    for x in range(SX):
        s = [shifted[i, x] for i in range(19)]
        density = s[0]
        momentum = [None, None, None]
        for i in range(1, 19, 2):
            density = density + (s[i] + s[i + 1])
            gap = s[i] - s[i + 1]
            for axis in range(3):
                c = VEL[i][axis]
                if c:
                    old = momentum[axis]
                    if old is None:
                        momentum[axis] = gap
                    else:
                        momentum[axis] = old + gap if c > 0 else old - gap
        push = [body[c, x] for c in range(3)]
        for c in range(3):
            force[c, x] = push[c]
        inverse = 1.0 / density
        flow = [(momentum[a] + 0.5 * push[a]) * inverse for a in range(3)]
        speed = flow[0] * flow[0] + flow[1] * flow[1] + flow[2] * flow[2]
        work = flow[0] * push[0] + flow[1] * push[1] + flow[2] * push[2]
        wall = solid[x] == 1
        common = density * (1.25 - 1.875 * speed) - 1.125 * work
        square = 5.625 * density
        linear = 3.75 * density
        new[0, x] = jnp.where(wall, s[0], (1.0 / 3.0) * common - 0.25 * s[0])
        for i in range(1, 19, 2):
            weight = 1.0 / 18.0 if i < 7 else 1.0 / 36.0
            a = b = None
            for axis in range(3):
                c = VEL[i][axis]
                if c:
                    if a is None:
                        a, b = flow[axis], push[axis]
                    elif c > 0:
                        a, b = a + flow[axis], b + push[axis]
                    else:
                        a, b = a - flow[axis], b - push[axis]
            even = weight * (common + a * (square * a + 3.375 * b))
            odd = weight * (linear * a + 1.125 * b)
            new[i, x] = jnp.where(wall, s[i + 1], (even + odd) - 0.25 * s[i])
            new[i + 1, x] = jnp.where(wall, s[i], (even - odd) - 0.25 * s[i + 1])


def whole(count):
    return [pl.BlockSpec(memory_space=pltpu.VMEM)] * count


def local(populations, solid_mask, displacement, stiffness, neighbours, owners, stencil_base, stencil_weights):
    def f32(*shape):
        return jax.ShapeDtypeStruct(shape, F32)

    def vmem(*shape):
        return pltpu.VMEM(shape, F32)

    halo = (2, 5, SY, SZ), (2, 5, SX, SZ), (2, 8, 128)
    shifted, body = pl.pallas_call(
        gather_kernel,
        out_shape=(f32(19, SX, SY, SZ), f32(3, SX, SY, SZ)),
        in_specs=[pl.BlockSpec(memory_space=pltpu.HBM)] + whole(6),
        out_specs=tuple(whole(2)),
        scratch_shapes=[
            vmem(19, SX, SY, SZ), vmem(4, 8, 1024), vmem(GROUP, 4, 128), vmem(GROUP, 4, 128),
            *(vmem(*shape) for shape in halo), *(vmem(*shape) for shape in halo),
            vmem(4, SX, SZ), vmem(4, SY, SZ), vmem(4, SX, SZ),
            vmem(16, 4, 4, 128), pltpu.VMEM((384, 256), BF16), pltpu.VMEM((256, 256), BF16), vmem(384, 256),
            pltpu.SemaphoreType.DMA,
            pltpu.SemaphoreType.DMA((GROUP,)),
            pltpu.SemaphoreType.DMA((GROUP,)),
            pltpu.SemaphoreType.DMA((18,)),
            pltpu.SemaphoreType.DMA((18,)),
            pltpu.SemaphoreType.REGULAR,
        ],
        compiler_params=pltpu.CompilerParams(
            collective_id=0, has_side_effects=True, vmem_limit_bytes=16 * 1024 * 1024
        ),
        name="gather",
    )(
        *(pltpu.with_memory_space_constraint(v, pltpu.HBM) for v in (
        populations, displacement, stiffness.reshape(1, 1024), neighbours,
        owners.reshape(1, 1024), stencil_base.reshape(1, 1024), stencil_weights))
    )
    return tuple(
        pl.pallas_call(
            collide_kernel,
            out_shape=(f32(19, SX, SY, SZ), f32(3, SX, SY, SZ)),
            in_specs=whole(3),
            out_specs=tuple(whole(2)),
            compiler_params=pltpu.CompilerParams(vmem_limit_bytes=8 * 1024 * 1024),
            name="collide",
        )(shifted, solid_mask, body)
    )


def solution(mesh):
    placed = (
        P(None, "gx", "gy", "gz"),
        P("gx", "gy", "gz"),
        P(None, ("gx", "gy", "gz")),
        P(("gx", "gy", "gz")),
        P(None, ("gx", "gy", "gz")),
        P(("gx", "gy", "gz"), None),
        P(("gx", "gy", "gz")),
        P(None, ("gx", "gy", "gz")),
    )
    return jax.shard_map(
        local,
        mesh=mesh,
        in_specs=placed,
        out_specs=(P(None, "gx", "gy", "gz"), P(None, "gx", "gy", "gz")),
        check_vma=False,
    )
```

time: 39.7 us -> 35.3 us (0.89)
  the two profiles are of different devices: /device:TPU:4 before, /device:TPU:256 now
where the time goes in v2:
time: 35.3 us; the launch traced here: 35 us
  Pallas kernels  34.4 us (97%)
  between operations  0.66 us (2%)
    pallas_call x1, Pallas kernels, local(): pl.pallas_call(gather_kernel, out_shape=(f32(19, SX, SY, SZ), f32(3, SX,...  33.3 us
    pallas_call x1, Pallas kernels, local(): pl.pallas_call(collide_kernel, out_shape=(f32(19, SX, SY, SZ), f32(3, SX,...  1.12 us

profile of v2, /device:TPU:256, one launch (start us, length us, event | category | flops | bytes accessed | tf_op | source)
XLA Modules:
  0.0 35.0 jit_solution(17189177549987325641)
XLA Ops:
  0.6 0.0 copy-start
  0.6 33.3 %gather.1 = (f32[19,4,16,128]{3,2,1,0:T(8,128)S(1)}, f32[3,4,16,128]{3,2,1,0:T(8,128)S(1)}) custom-call(f32[19,4,16,128]{3,2,1,0:T(8,128)} %pop_hbm.1, f32[3,1024]{1,0:T(4,128)} %disp.1, f32[1,1024]{1,0:T(1,128)} %bitcast.3, s32[6,1024]{1,0:T(8,128)} %nbr.1, s32[1,1024]{1,0:T(1,128)} %bitcast.4, s32[1,1024]{1,0:T(1,128)} %bitcast.5, f32[12,1024]{1,0:T(8,128)} %weights.1), custom_call_target="tpu_custom_call" | custom-call | tf_op jit(solution)/shard_map/gather/pallas_call | solution.py:454
  33.9 0.0 copy-done
  33.9 1.1 %collide.1 = (f32[19,4,16,128]{3,2,1,0:T(8,128)}, f32[3,4,16,128]{3,2,1,0:T(8,128)}) custom-call(f32[19,4,16,128]{3,2,1,0:T(8,128)S(1)} %get-tuple-element.4.shifted, s32[4,16,128]{2,1,0:T(8,128)S(1)} %copy-done, f32[3,4,16,128]{3,2,1,0:T(8,128)S(1)} %get-tuple-element.5.body), custom_call_target="tpu_custom_call" | custom-call | tf_op jit(solution)/shard_map/collide/pallas_call | solution.py:481
Async XLA Ops:
  0.6 33.3 %copy-start = (s32[4,16,128]{2,1,0:T(8,128)S(1)}, s32[4,16,128]{2,1,0:T(8,128)}, u32[]{:S(2)}) copy-start(s32[4,16,128]{2,1,0:T(8,128)} %solid.1) | copy-start | bytes 98308

commit v3 on v2

--- a/solution.py
+++ b/solution.py
@@ -256,7 +256,7 @@
     pop_hbm, disp, stiff, nbr, owner, base, weights, shifted, force,
     pop, pay, send, got, hx, hy, hz, got_hx, got_hy, got_hz, got_xy, got_xz, got_yz,
     quads, left, table, total,
-    load_sem, send_sem, recv_sem, halo_send, halo_recv, late_sem,
+    load_sem, send_sem, recv_sem, halo_send, halo_recv, late_sem, go_sem, edge_sem,
 ):
     gx, gy, gz = lax.axis_index("gx"), lax.axis_index("gy"), lax.axis_index("gz")
     me = gy * N_GZ + gz
@@ -281,23 +281,41 @@
         for t in range(1, GROUP):
             signal(barrier, place(0, t // N_GZ, t % N_GZ))
 
+    def far(step):
+        return lax.rem(gz + step[2] + N_GZ, N_GZ) >= 4
+
+    def all_of(*terms):
+        return functools.reduce(jnp.logical_and, terms)
+
     for step in outside:
-        signal(barrier, place(*step))
+        if step[2]:
+            pl.when(jnp.logical_or(first, far(step)))(functools.partial(signal, barrier, place(*step)))
+        else:
+            signal(barrier, place(*step))
     load = pltpu.make_async_copy(pop_hbm, pop, load_sem)
     load.start()
 
     pack_vertices(disp, stiff, nbr, owner, base, weights, send, pay)
 
-    @pl.when(first)
+    rim = jnp.logical_or(gz == 0, gz == 3)
+
+    @pl.when(rim)
+    def _():
+        pl.semaphore_wait(barrier, 31 + len(outside) - 2)
+
+    @pl.when(all_of(first, jnp.logical_not(rim)))
     def _():
         pl.semaphore_wait(barrier, 31 + len(outside))
 
     @pl.when(jnp.logical_not(first))
     def _():
         pl.semaphore_wait(barrier, 32 + len(outside))
-        for k in range(8):
-            for z in range(4):
+        for z in range(4):
+            for k in range(8):
                 signal(late_sem, {"gx": gx, "gy": lax.rem(gy + k, N_GY), "gz": z})
+        for step in outside:
+            if step[2]:
+                pl.when(jnp.logical_not(far(step)))(functools.partial(signal, edge_sem, place(*step)))
 
     def vertex_copy(y, z):
         index = y * N_GZ + z
@@ -331,16 +349,24 @@
             )
         )
 
-    def start_halos(late):
+    for (step, _, _), copy in zip(messages, halos):
+        if step[0] and not step[2]:
+            copy.start()
+        elif step[0]:
+            pl.when(jnp.logical_not(all_of(first, far(step))))(copy.start)
+        else:
+            pl.when(jnp.logical_not(far(step)))(copy.start)
+
+    def send_to_late():
+        vertex_copies(range(4, 8), lambda copy: copy.start())
         for (step, _, _), copy in zip(messages, halos):
-            if step[0]:
-                if not late:
-                    copy.start()
-            else:
-                near = lax.rem(gz + step[2] + N_GZ, N_GZ) < 4
-                pl.when(jnp.logical_not(near) if late else near)(copy.start)
-
-    start_halos(False)
+            if not step[0]:
+                pl.when(far(step))(copy.start)
+
+    @pl.when(jnp.logical_not(first))
+    def _():
+        pl.semaphore_wait(go_sem, 1)
+        send_to_late()
 
     def arrived(y, z):
         index = y * N_GZ + z
@@ -361,9 +387,15 @@
     @pl.when(first)
     def _():
         pl.semaphore_wait(late_sem, 32)
-
-    vertex_copies(range(4, 8), lambda copy: copy.start())
-    start_halos(True)
+        signal(go_sem, {"gx": gx, "gy": gy, "gz": gz + 4})
+        send_to_late()
+
+    @pl.when(rim)
+    def _():
+        pl.semaphore_wait(edge_sem, 2)
+        for (step, _, _), copy in zip(messages, halos):
+            if step[0] and step[2]:
+                pl.when(far(step))(copy.start)
 
     for copy in halos:
         copy.wait_recv()
@@ -467,6 +499,8 @@
             pltpu.SemaphoreType.DMA((18,)),
             pltpu.SemaphoreType.DMA((18,)),
             pltpu.SemaphoreType.REGULAR,
+            pltpu.SemaphoreType.REGULAR,
+            pltpu.SemaphoreType.REGULAR,
         ],
         compiler_params=pltpu.CompilerParams(
             collective_id=0, has_side_effects=True, vmem_limit_bytes=16 * 1024 * 1024

time: 35.3 us -> 28.5 us (0.81)
  Pallas kernels: 34.4 us -> 27.6 us
    pallas_call x1, Pallas kernels: 33.3 us -> 26.5 us  [local(): pl.pallas_call(gather_kernel, out_shape=(f32(19, SX, SY, SZ), f32(3, SX,...]
where the time goes in v3:
time: 28.5 us; the launch traced here: 28.2 us
  Pallas kernels  27.6 us (97%)
  between operations  0.66 us (2%)
    pallas_call x1, Pallas kernels, local(): pl.pallas_call(gather_kernel, out_shape=(f32(19, SX, SY, SZ), f32(3, SX,...  26.5 us
    pallas_call x1, Pallas kernels, local(): pl.pallas_call(collide_kernel, out_shape=(f32(19, SX, SY, SZ), f32(3, SX,...  1.12 us

profile of v3, /device:TPU:256, one launch (start us, length us, event | category | flops | bytes accessed | tf_op | source)
XLA Modules:
  0.0 28.2 jit_solution(1167368209180842424)
XLA Ops:
  0.6 0.0 copy-start
  0.6 26.5 %gather.1 = (f32[19,4,16,128]{3,2,1,0:T(8,128)S(1)}, f32[3,4,16,128]{3,2,1,0:T(8,128)S(1)}) custom-call(f32[19,4,16,128]{3,2,1,0:T(8,128)} %pop_hbm.1, f32[3,1024]{1,0:T(4,128)} %disp.1, f32[1,1024]{1,0:T(1,128)} %bitcast.3, s32[6,1024]{1,0:T(8,128)} %nbr.1, s32[1,1024]{1,0:T(1,128)} %bitcast.4, s32[1,1024]{1,0:T(1,128)} %bitcast.5, f32[12,1024]{1,0:T(8,128)} %weights.1), custom_call_target="tpu_custom_call" | custom-call | tf_op jit(solution)/shard_map/gather/pallas_call | solution.py:486
  27.1 0.0 copy-done
  27.1 1.1 %collide.1 = (f32[19,4,16,128]{3,2,1,0:T(8,128)}, f32[3,4,16,128]{3,2,1,0:T(8,128)}) custom-call(f32[19,4,16,128]{3,2,1,0:T(8,128)S(1)} %get-tuple-element.4.shifted, s32[4,16,128]{2,1,0:T(8,128)S(1)} %copy-done, f32[3,4,16,128]{3,2,1,0:T(8,128)S(1)} %get-tuple-element.5.body), custom_call_target="tpu_custom_call" | custom-call | tf_op jit(solution)/shard_map/collide/pallas_call | solution.py:515
Async XLA Ops:
  0.6 26.5 %copy-start = (s32[4,16,128]{2,1,0:T(8,128)S(1)}, s32[4,16,128]{2,1,0:T(8,128)}, u32[]{:S(2)}) copy-start(s32[4,16,128]{2,1,0:T(8,128)} %solid.1) | copy-start | bytes 98308

commit v4 on v2

--- a/solution.py
+++ b/solution.py
@@ -22,6 +22,7 @@
 )
 SX, SY, SZ = 4, 16, 128
 N_GY = N_GZ = 8
+EARLY = 2
 GROUP = N_GY * N_GZ
 FACE = tuple(
     tuple(tuple(i for i in range(19) if VEL[i][axis] == sign) for sign in (1, -1))
@@ -229,7 +230,8 @@
                 line = jnp.where(masks["z4", cz], beyond, line)
         else:
             line = exy[EDGE_XY.index(i)]
-        line = line[source % SX : source % SX + 1]
+        row = source if inside else (7 if cy > 0 else 0)
+        line = line[row : row + 1]
         cells = jnp.where(masks["y", cy], jnp.broadcast_to(line, (SY, SZ)), cells)
     return cells
 
@@ -241,11 +243,10 @@
         messages.append(((0, sign, 0), hy.at[s], got_hy.at[s]))
         messages.append(((0, 0, sign), hz.at[s], got_hz.at[s]))
     for n, i in enumerate(EDGE_XY):
-        s, k = face_slot(1, i)
-        messages.append((VEL[i], hy.at[s, k], got_xy.at[n]))
+        half = 8 if VEL[i][1] > 0 else 0
+        messages.append(((0, VEL[i][1], 0), got_hx.at[face_slot(0, i)].at[pl.ds(half, 8)], got_xy.at[n]))
     for n, i in enumerate(EDGE_XZ):
-        s, k = face_slot(0, i)
-        messages.append((VEL[i], hx.at[s, k], got_xz.at[n]))
+        messages.append(((0, 0, VEL[i][2]), got_hx.at[face_slot(0, i)], got_xz.at[n]))
     for n, i in enumerate(EDGE_YZ):
         s, k = face_slot(1, i)
         messages.append((VEL[i], hy.at[s, k], got_yz.at[n]))
@@ -253,14 +254,14 @@
 
 
 def gather_kernel(
-    pop_hbm, disp, stiff, nbr, owner, base, weights, shifted, force,
-    pop, pay, send, got, hx, hy, hz, got_hx, got_hy, got_hz, got_xy, got_xz, got_yz,
+    pop_in, disp_in, stiff_in, nbr_in, owner_in, base_in, weights_in,
+    shifted, force, pop, disp, stiff, nbr, owner, base, weights, pay, send, got, hx, hy, hz, got_hx, got_hy, got_hz, got_xy, got_xz, got_yz,
     quads, left, table, total,
-    load_sem, send_sem, recv_sem, halo_send, halo_recv, late_sem,
+    load_sem, send_sem, recv_sem, halo_send, halo_recv, late_sem, go_sem,
 ):
     gx, gy, gz = lax.axis_index("gx"), lax.axis_index("gy"), lax.axis_index("gz")
     me = gy * N_GZ + gz
-    first = gz < 4
+    first = gz < EARLY
 
     def place(dx, dy, dz):
         return {
@@ -281,23 +282,32 @@
         for t in range(1, GROUP):
             signal(barrier, place(0, t // N_GZ, t % N_GZ))
 
+    def far(step):
+        return lax.rem(gz + step[2] + N_GZ, N_GZ) >= EARLY
+
     for step in outside:
         signal(barrier, place(*step))
-    load = pltpu.make_async_copy(pop_hbm, pop, load_sem)
-    load.start()
-
+    pairs = (
+        (disp_in, disp), (nbr_in, nbr), (owner_in, owner), (stiff_in, stiff), (base_in, base),
+        (weights_in, weights), (pop_in, pop),
+    )
+    loads = [pltpu.make_async_copy(src, dst, load_sem.at[n]) for n, (src, dst) in enumerate(pairs)]
+    for copy in loads:
+        copy.start()
+    for copy in loads[:-1]:
+        copy.wait()
     pack_vertices(disp, stiff, nbr, owner, base, weights, send, pay)
 
     @pl.when(first)
     def _():
-        pl.semaphore_wait(barrier, 31 + len(outside))
+        pl.semaphore_wait(barrier, N_GY * EARLY - 1 + len(outside))
 
     @pl.when(jnp.logical_not(first))
     def _():
-        pl.semaphore_wait(barrier, 32 + len(outside))
-        for k in range(8):
-            for z in range(4):
-                signal(late_sem, {"gx": gx, "gy": lax.rem(gy + k, N_GY), "gz": z})
+        pl.semaphore_wait(barrier, N_GY * EARLY + len(outside))
+        for z in range(EARLY):
+            for k in range(8):
+                signal(late_sem.at[me], {"gx": gx, "gy": lax.rem(gy + k, N_GY), "gz": z})
 
     def vertex_copy(y, z):
         index = y * N_GZ + z
@@ -309,18 +319,18 @@
 
     def vertex_copies(planes, act):
         for z in planes:
-            for k in range(8):
+            for k in (4, 3, 5, 2, 6, 1, 7, 0):
                 copy = vertex_copy(lax.rem(gy + k, N_GY), z)
                 if k:
                     act(copy)
                 else:
                     pl.when(gz != z)(functools.partial(act, copy))
 
-    vertex_copies(range(0, 4), lambda copy: copy.start())
+    vertex_copies(range(EARLY), lambda copy: copy.start())
     own = pltpu.make_async_copy(send.at[me], got.at[me], recv_sem.at[me])
     own.start()
 
-    load.wait()
+    loads[-1].wait()
     pack_faces(pop, hx, hy, hz)
     halos = []
     for n, (step, src, dst) in enumerate(messages):
@@ -331,16 +341,67 @@
             )
         )
 
-    def start_halos(late):
-        for (step, _, _), copy in zip(messages, halos):
-            if step[0]:
-                if not late:
-                    copy.start()
-            else:
-                near = lax.rem(gz + step[2] + N_GZ, N_GZ) < 4
-                pl.when(jnp.logical_not(near) if late else near)(copy.start)
-
-    start_halos(False)
+    passed_on = [6 <= n < 14 for n in range(len(messages))]
+
+    def near_halos(again):
+        for n, ((step, _, _), copy) in enumerate(zip(messages, halos)):
+            if not step[0] and passed_on[n] == again:
+                pl.when(jnp.logical_not(far(step)))(copy.start)
+
+    for copy in halos[0], halos[3]:
+        copy.start()
+    near_halos(False)
+    for copy in halos[0], halos[3]:
+        copy.wait_recv()
+    near_halos(True)
+
+    def halos_to(z):
+        for dz in (-1, 0, 1):
+
+            @pl.when(lax.rem(gz + dz + N_GZ, N_GZ) == z)
+            def _():
+                for (step, _, _), copy in zip(messages, halos):
+                    if step[0] == 0 and step[2] == dz:
+                        copy.start()
+
+    def serve(z, rows):
+        for k in rows:
+            y = lax.rem(gy + k, N_GY)
+            pl.semaphore_wait(late_sem.at[y * N_GZ + z], 1)
+            vertex_copy(y, z).start()
+
+    def pass_on(z):
+        for j in range(3):
+            signal(go_sem.at[z], {"gx": gx, "gy": gy, "gz": 7 - j + gz * (2 * j - 5)})
+
+    def own_row(planes, brick):
+        @pl.when(gz == brick)
+        def _():
+            for z in planes:
+                serve(z, (0,))
+
+    near_rows, far_rows = (1, 7, 2, 6), (3, 5, 4)
+
+    @pl.when(first)
+    def _():
+        own_row(range(2, 5), 1)
+        own_row(range(5, 8), 0)
+        for z in range(EARLY, 4):
+            own_row([z], 0)
+            serve(z, near_rows + far_rows)
+            pass_on(z)
+            halos_to(z)
+        for z in range(4, 8):
+            own_row([z], 0 if z == 4 else 1)
+            serve(z, near_rows)
+            halos_to(z)
+
+    @pl.when(jnp.logical_not(first))
+    def _():
+        for z in range(EARLY, 8):
+            pl.semaphore_wait(go_sem.at[z], 1)
+            vertex_copies([z], lambda copy: copy.start())
+            halos_to(z)
 
     def arrived(y, z):
         index = y * N_GZ + z
@@ -355,18 +416,18 @@
         return spread_step(got, [2 * y + half for y in order[n]], quads, left, table)
 
     total[...] = step(0, 0)
+
+    @pl.when(first)
+    def _():
+        for z in range(4, 8):
+            serve(z, far_rows)
+            pass_on(z)
+
     for n in range(1, 4):
         total[...] += step(n, 0)
-
-    @pl.when(first)
-    def _():
-        pl.semaphore_wait(late_sem, 32)
-
-    vertex_copies(range(4, 8), lambda copy: copy.start())
-    start_halos(True)
-
-    for copy in halos:
-        copy.wait_recv()
+    for n, copy in enumerate(halos):
+        if n not in (0, 3):
+            copy.wait_recv()
     lane = lax.broadcasted_iota(I32, (SY, SZ), 1)
     line = lax.broadcasted_iota(I32, (SY, SZ), 0)
     lane4 = lax.broadcasted_iota(I32, (SX, SZ), 1)
@@ -393,7 +454,9 @@
             force[c, x] = field[spot : spot + SY]
 
 
-def collide_kernel(shifted, solid, body, new, force):
+def collide_kernel(shifted, solid, body, new_out, force_out, new, sems):
+    copies = [pltpu.make_async_copy(body, force_out, sems.at[SX])]
+    copies[0].start()
     for x in range(SX):
         s = [shifted[i, x] for i in range(19)]
         density = s[0]
@@ -410,8 +473,6 @@
                     else:
                         momentum[axis] = old + gap if c > 0 else old - gap
         push = [body[c, x] for c in range(3)]
-        for c in range(3):
-            force[c, x] = push[c]
         inverse = 1.0 / density
         flow = [(momentum[a] + 0.5 * push[a]) * inverse for a in range(3)]
         speed = flow[0] * flow[0] + flow[1] * flow[1] + flow[2] * flow[2]
@@ -437,6 +498,10 @@
             odd = weight * (linear * a + 1.125 * b)
             new[i, x] = jnp.where(wall, s[i + 1], (even + odd) - 0.25 * s[i])
             new[i + 1, x] = jnp.where(wall, s[i], (even - odd) - 0.25 * s[i + 1])
+        copies.append(pltpu.make_async_copy(new.at[:, x], new_out.at[:, x], sems.at[x]))
+        copies[-1].start()
+    for copy in copies:
+        copy.wait()
 
 
 def whole(count):
@@ -454,19 +519,21 @@
     shifted, body = pl.pallas_call(
         gather_kernel,
         out_shape=(f32(19, SX, SY, SZ), f32(3, SX, SY, SZ)),
-        in_specs=[pl.BlockSpec(memory_space=pltpu.HBM)] + whole(6),
+        in_specs=[pl.BlockSpec(memory_space=pltpu.HBM)] * 7,
         out_specs=tuple(whole(2)),
         scratch_shapes=[
-            vmem(19, SX, SY, SZ), vmem(4, 8, 1024), vmem(GROUP, 4, 128), vmem(GROUP, 4, 128),
+            vmem(19, SX, SY, SZ), vmem(3, 1024), vmem(1, 1024), pltpu.VMEM((6, 1024), I32), pltpu.VMEM((1, 1024), I32),
+            pltpu.VMEM((1, 1024), I32), vmem(12, 1024), vmem(4, 8, 1024), vmem(GROUP, 4, 128), vmem(GROUP, 4, 128),
             *(vmem(*shape) for shape in halo), *(vmem(*shape) for shape in halo),
-            vmem(4, SX, SZ), vmem(4, SY, SZ), vmem(4, SX, SZ),
+            vmem(4, 8, SZ), vmem(4, SY, SZ), vmem(4, SX, SZ),
             vmem(16, 4, 4, 128), pltpu.VMEM((384, 256), BF16), pltpu.VMEM((256, 256), BF16), vmem(384, 256),
-            pltpu.SemaphoreType.DMA,
+            pltpu.SemaphoreType.DMA((7,)),
             pltpu.SemaphoreType.DMA((GROUP,)),
             pltpu.SemaphoreType.DMA((GROUP,)),
             pltpu.SemaphoreType.DMA((18,)),
             pltpu.SemaphoreType.DMA((18,)),
-            pltpu.SemaphoreType.REGULAR,
+            pltpu.SemaphoreType.REGULAR((GROUP,)),
+            pltpu.SemaphoreType.REGULAR((N_GZ,)),
         ],
         compiler_params=pltpu.CompilerParams(
             collective_id=0, has_side_effects=True, vmem_limit_bytes=16 * 1024 * 1024
@@ -482,7 +549,8 @@
             collide_kernel,
             out_shape=(f32(19, SX, SY, SZ), f32(3, SX, SY, SZ)),
             in_specs=whole(3),
-            out_specs=tuple(whole(2)),
+            out_specs=(pl.BlockSpec(memory_space=pltpu.HBM),) * 2,
+            scratch_shapes=[vmem(19, SX, SY, SZ), pltpu.SemaphoreType.DMA((SX + 1,))],
             compiler_params=pltpu.CompilerParams(vmem_limit_bytes=8 * 1024 * 1024),
             name="collide",
         )(shifted, solid_mask, body)

time: 35.3 us -> 25.8 us (0.73)
  the two profiles are of different devices: /device:TPU:256 before, /device:TPU:128 now
where the time goes in v4:
time: 25.8 us; the launch traced here: 25.7 us
  Pallas kernels  25 us (97%)
  between operations  0.66 us (3%)
    pallas_call x1, Pallas kernels, local(): pl.pallas_call(gather_kernel, out_shape=(f32(19, SX, SY, SZ), f32(3, SX,...  24 us
    pallas_call x1, Pallas kernels, local(): pl.pallas_call(collide_kernel, out_shape=(f32(19, SX, SY, SZ), f32(3, SX,...  1 us

profile of v4, /device:TPU:128, one launch (start us, length us, event | category | flops | bytes accessed | tf_op | source)
XLA Modules:
  0.0 25.7 jit_solution(9396414077835579956)
XLA Ops:
  0.6 0.0 copy-start
  0.6 24.0 %gather.1 = (f32[19,4,16,128]{3,2,1,0:T(8,128)S(1)}, f32[3,4,16,128]{3,2,1,0:T(8,128)S(1)}) custom-call(f32[19,4,16,128]{3,2,1,0:T(8,128)} %pop_in.1, f32[3,1024]{1,0:T(4,128)} %disp_in.1, f32[1,1024]{1,0:T(1,128)} %bitcast.3, s32[6,1024]{1,0:T(8,128)} %nbr_in.1, s32[1,1024]{1,0:T(1,128)} %bitcast.4, s32[1,1024]{1,0:T(1,128)} %bitcast.5, f32[12,1024]{1,0:T(8,128)} %weights_in.1), custom_call_target="tpu_custom_call" | custom-call | tf_op jit(solution)/shard_map/gather/pallas_call | solution.py:519
  24.7 0.0 copy-done
  24.7 1.0 %collide.1 = (f32[19,4,16,128]{3,2,1,0:T(8,128)}, f32[3,4,16,128]{3,2,1,0:T(8,128)}) custom-call(f32[19,4,16,128]{3,2,1,0:T(8,128)S(1)} %get-tuple-element.4.shifted, s32[4,16,128]{2,1,0:T(8,128)S(1)} %copy-done, f32[3,4,16,128]{3,2,1,0:T(8,128)S(1)} %get-tuple-element.5.body), custom_call_target="tpu_custom_call" | custom-call | tf_op jit(solution)/shard_map/collide/pallas_call | solution.py:548
Async XLA Ops:
  0.6 24.0 %copy-start = (s32[4,16,128]{2,1,0:T(8,128)S(1)}, s32[4,16,128]{2,1,0:T(8,128)}, u32[]{:S(2)}) copy-start(s32[4,16,128]{2,1,0:T(8,128)} %solid.1) | copy-start | bytes 98308

commit v5 on v4

--- a/solution.py
+++ b/solution.py
@@ -22,7 +22,7 @@
 )
 SX, SY, SZ = 4, 16, 128
 N_GY = N_GZ = 8
-EARLY = 2
+EARLY = 3
 GROUP = N_GY * N_GZ
 FACE = tuple(
     tuple(tuple(i for i in range(19) if VEL[i][axis] == sign) for sign in (1, -1))
@@ -296,18 +296,20 @@
         copy.start()
     for copy in loads[:-1]:
         copy.wait()
+    def announce():
+        pl.semaphore_wait(barrier, N_GY * EARLY + len(outside))
+        for z in range(EARLY):
+            for k in (4, 3, 5, 2, 6, 1, 7, 0):
+                signal(late_sem.at[me], {"gx": gx, "gy": lax.rem(gy + k, N_GY), "gz": z})
+
+    slow = jnp.logical_or(gx == 0, gy < 2)
+    pl.when(jnp.logical_not(jnp.logical_or(first, slow)))(announce)
     pack_vertices(disp, stiff, nbr, owner, base, weights, send, pay)
+    pl.when(jnp.logical_and(jnp.logical_not(first), slow))(announce)
 
     @pl.when(first)
     def _():
         pl.semaphore_wait(barrier, N_GY * EARLY - 1 + len(outside))
-
-    @pl.when(jnp.logical_not(first))
-    def _():
-        pl.semaphore_wait(barrier, N_GY * EARLY + len(outside))
-        for z in range(EARLY):
-            for k in range(8):
-                signal(late_sem.at[me], {"gx": gx, "gy": lax.rem(gy + k, N_GY), "gz": z})
 
     def vertex_copy(y, z):
         index = y * N_GZ + z
@@ -326,7 +328,7 @@
                 else:
                     pl.when(gz != z)(functools.partial(act, copy))
 
-    vertex_copies(range(EARLY), lambda copy: copy.start())
+    vertex_copies([0], lambda copy: copy.start())
     own = pltpu.make_async_copy(send.at[me], got.at[me], recv_sem.at[me])
     own.start()
 
@@ -350,6 +352,7 @@
 
     for copy in halos[0], halos[3]:
         copy.start()
+    vertex_copies(range(1, EARLY), lambda copy: copy.start())
     near_halos(False)
     for copy in halos[0], halos[3]:
         copy.wait_recv()
@@ -370,29 +373,39 @@
             pl.semaphore_wait(late_sem.at[y * N_GZ + z], 1)
             vertex_copy(y, z).start()
 
+    words = ((EARLY - 1, (3, 4)), (0, (7, 6, 5)))
+
     def pass_on(z):
-        for j in range(3):
-            signal(go_sem.at[z], {"gx": gx, "gy": gy, "gz": 7 - j + gz * (2 * j - 5)})
-
-    def own_row(planes, brick):
-        @pl.when(gz == brick)
-        def _():
-            for z in planes:
-                serve(z, (0,))
+        for brick, planes in words:
+
+            @pl.when(gz == brick)
+            def _():
+                for to in planes:
+                    signal(go_sem.at[z], {"gx": gx, "gy": gy, "gz": to})
+
+    def rest_of_own_row(z):
+        for brick, planes in words:
+            if z in planes:
+                pl.when(gz != brick)(lambda: serve(z, (0,)))
 
     near_rows, far_rows = (1, 7, 2, 6), (3, 5, 4)
 
     @pl.when(first)
     def _():
-        own_row(range(2, 5), 1)
-        own_row(range(5, 8), 0)
+        for brick, planes in words:
+
+            @pl.when(gz == brick)
+            def _():
+                for z in planes:
+                    serve(z, (0,))
+
         for z in range(EARLY, 4):
-            own_row([z], 0)
+            rest_of_own_row(z)
             serve(z, near_rows + far_rows)
             pass_on(z)
             halos_to(z)
         for z in range(4, 8):
-            own_row([z], 0 if z == 4 else 1)
+            rest_of_own_row(z)
             serve(z, near_rows)
             halos_to(z)
 

time: 25.8 us -> 25.5 us (0.988)
  the two profiles are of different devices: /device:TPU:128 before, /device:TPU:1 now
where the time goes in v5:
time: 25.5 us; the launch traced here: 25.4 us
  Pallas kernels  24.7 us (97%)
  between operations  0.66 us (3%)
    pallas_call x1, Pallas kernels, local(): pl.pallas_call(gather_kernel, out_shape=(f32(19, SX, SY, SZ), f32(3, SX,...  23.7 us
    pallas_call x1, Pallas kernels, local(): pl.pallas_call(collide_kernel, out_shape=(f32(19, SX, SY, SZ), f32(3, SX,...  1 us

profile of v5, /device:TPU:1, one launch (start us, length us, event | category | flops | bytes accessed | tf_op | source)
XLA Modules:
  0.0 25.4 jit_solution(7366705051121481120)
XLA Ops:
  0.6 0.0 copy-start
  0.6 23.7 %gather.1 = (f32[19,4,16,128]{3,2,1,0:T(8,128)S(1)}, f32[3,4,16,128]{3,2,1,0:T(8,128)S(1)}) custom-call(f32[19,4,16,128]{3,2,1,0:T(8,128)} %pop_in.1, f32[3,1024]{1,0:T(4,128)} %disp_in.1, f32[1,1024]{1,0:T(1,128)} %bitcast.3, s32[6,1024]{1,0:T(8,128)} %nbr_in.1, s32[1,1024]{1,0:T(1,128)} %bitcast.4, s32[1,1024]{1,0:T(1,128)} %bitcast.5, f32[12,1024]{1,0:T(8,128)} %weights_in.1), custom_call_target="tpu_custom_call" | custom-call | tf_op jit(solution)/shard_map/gather/pallas_call | solution.py:532
  24.3 0.0 copy-done
  24.3 1.0 %collide.1 = (f32[19,4,16,128]{3,2,1,0:T(8,128)}, f32[3,4,16,128]{3,2,1,0:T(8,128)}) custom-call(f32[19,4,16,128]{3,2,1,0:T(8,128)S(1)} %get-tuple-element.4.shifted, s32[4,16,128]{2,1,0:T(8,128)S(1)} %copy-done, f32[3,4,16,128]{3,2,1,0:T(8,128)S(1)} %get-tuple-element.5.body), custom_call_target="tpu_custom_call" | custom-call | tf_op jit(solution)/shard_map/collide/pallas_call | solution.py:561
Async XLA Ops:
  0.6 23.7 %copy-start = (s32[4,16,128]{2,1,0:T(8,128)S(1)}, s32[4,16,128]{2,1,0:T(8,128)}, u32[]{:S(2)}) copy-start(s32[4,16,128]{2,1,0:T(8,128)} %solid.1) | copy-start | bytes 98308

commit v6 on v5

--- a/solution.py
+++ b/solution.py
@@ -302,7 +302,7 @@
             for k in (4, 3, 5, 2, 6, 1, 7, 0):
                 signal(late_sem.at[me], {"gx": gx, "gy": lax.rem(gy + k, N_GY), "gz": z})
 
-    slow = jnp.logical_or(gx == 0, gy < 2)
+    slow = jnp.logical_or(gx == 0, jnp.logical_or(gy < 2, gy == 7))
     pl.when(jnp.logical_not(jnp.logical_or(first, slow)))(announce)
     pack_vertices(disp, stiff, nbr, owner, base, weights, send, pay)
     pl.when(jnp.logical_and(jnp.logical_not(first), slow))(announce)
@@ -352,8 +352,8 @@
 
     for copy in halos[0], halos[3]:
         copy.start()
+    near_halos(False)
     vertex_copies(range(1, EARLY), lambda copy: copy.start())
-    near_halos(False)
     for copy in halos[0], halos[3]:
         copy.wait_recv()
     near_halos(True)

time: 25.5 us -> 25.5 us (level)
  no operation moved by 1% of the time
where the time goes in v6:
time: 25.5 us; the launch traced here: 25.3 us
  Pallas kernels  24.7 us (97%)
  between operations  0.66 us (3%)
    pallas_call x1, Pallas kernels, local(): pl.pallas_call(gather_kernel, out_shape=(f32(19, SX, SY, SZ), f32(3, SX,...  23.7 us
    pallas_call x1, Pallas kernels, local(): pl.pallas_call(collide_kernel, out_shape=(f32(19, SX, SY, SZ), f32(3, SX,...  1 us

profile of v6, /device:TPU:1, one launch (start us, length us, event | category | flops | bytes accessed | tf_op | source)
XLA Modules:
  0.0 25.3 jit_solution(11719123379418060205)
XLA Ops:
  0.6 0.0 copy-start
  0.6 23.7 %gather.1 = (f32[19,4,16,128]{3,2,1,0:T(8,128)S(1)}, f32[3,4,16,128]{3,2,1,0:T(8,128)S(1)}) custom-call(f32[19,4,16,128]{3,2,1,0:T(8,128)} %pop_in.1, f32[3,1024]{1,0:T(4,128)} %disp_in.1, f32[1,1024]{1,0:T(1,128)} %bitcast.3, s32[6,1024]{1,0:T(8,128)} %nbr_in.1, s32[1,1024]{1,0:T(1,128)} %bitcast.4, s32[1,1024]{1,0:T(1,128)} %bitcast.5, f32[12,1024]{1,0:T(8,128)} %weights_in.1), custom_call_target="tpu_custom_call" | custom-call | tf_op jit(solution)/shard_map/gather/pallas_call | solution.py:532
  24.3 0.0 copy-done
  24.3 1.0 %collide.1 = (f32[19,4,16,128]{3,2,1,0:T(8,128)}, f32[3,4,16,128]{3,2,1,0:T(8,128)}) custom-call(f32[19,4,16,128]{3,2,1,0:T(8,128)S(1)} %get-tuple-element.4.shifted, s32[4,16,128]{2,1,0:T(8,128)S(1)} %copy-done, f32[3,4,16,128]{3,2,1,0:T(8,128)S(1)} %get-tuple-element.5.body), custom_call_target="tpu_custom_call" | custom-call | tf_op jit(solution)/shard_map/collide/pallas_call | solution.py:561
Async XLA Ops:
  0.6 23.7 %copy-start = (s32[4,16,128]{2,1,0:T(8,128)S(1)}, s32[4,16,128]{2,1,0:T(8,128)}, u32[]{:S(2)}) copy-start(s32[4,16,128]{2,1,0:T(8,128)} %solid.1) | copy-start | bytes 98308
